TPU v7x, 32 devices: a whole 2x2x4 slice. The times are simulated.
32 devices in a mesh: grp: 2 (over y), tile: 8 (over z, x), ch: 2 (over core).
Axes of the slice: x: 2, y: 2, z: 4, core: 2. Of those that a mesh axis runs over, the one named last changes fastest.
Arguments:
- source: bfloat16 [64, 131072], P('ch', ('grp', 'tile')), parts along dimension 1, may hold values from -6 to 6
- request_rows: int32 [8, 8, 2048], P('tile'), may hold values from 0 to 8191, as said below
- cell_slots: int32 [8, 4, 4096], P('tile'), may hold values from 0 to 16383, as said below
- cell_counts: int32 [8, 4, 4096], P('tile'), may hold values from 1 to 16
- seam: int32 [8, 4], replicated, may hold values from 0 to 7
- conv_first: bfloat16 [3, 3, 128, 64], P(None, None, 'ch'), may hold values from -0.25 to 0.25
- bias_first: float32 [128], P('ch'), may hold values from -3 to 3
- conv_second: bfloat16 [3, 3, 64, 128], replicated, may hold values from -0.1875 to 0.1875
- bias_second: float32 [64], replicated, may hold values from -3 to 3
Outputs:
- forecast: bfloat16 [16, 64, 4096], P(('grp', 'tile'), 'ch'), parts along dimension 0
There are 2 independent parts, one for each index of `grp`. A program takes and returns all parts, laid end to end along the dimension named above; an argument that names none is the same for every part. Nothing has to cross between parts.
Inputs may be any that keep to these rules, and one draw needn't show every extreme that they name: request_rows[t, s, j] is a row among the 8192 source cells held at tile index s. cell_slots[t, k, p] names the column s * 2048 + j of fetched[t].
All inputs are finite; a program needn't handle non-finite values.
Results may differ from a plain program's by a relative error of at most 0.0047.
Values may be sent and summed in bfloat16 or wider, within the bound.
A program may use at most 64 MiB of HBM per device.

v0:
```python
import math

import jax
import jax.numpy as jnp
from jax import lax
from jax.sharding import PartitionSpec as P

SIDE = 64
TILE_ROW = 4


def from_behind(x, axis, by):
    size = lax.axis_size(axis)
    return lax.ppermute(x, axis, [(i, (i + by) % size) for i in range(size)])


def remap_cells(fetched, slot_table, counts):
    weights = counts.astype(jnp.float32)
    count_total = weights[0]
    for entry in range(1, slot_table.shape[0]):
        count_total = count_total + weights[entry]
    weighted = None
    for entry in range(slot_table.shape[0]):
        picked = jnp.take(fetched, slot_table[entry], axis=1).astype(jnp.float32)
        contribution = weights[entry][None, :] * picked
        weighted = contribution if weighted is None else weighted + contribution
    return (weighted / count_total[None, :]).astype(jnp.bfloat16)


def orient(rim_edges, seam_code):
    chosen = lax.dynamic_index_in_dim(rim_edges, seam_code % 4, 0, keepdims=False)
    return jnp.where(seam_code >= 4, chosen[:, ::-1], chosen)


def assemble(field_grid, north_rim, east_rim, south_rim, west_rim):

    def corner(first_rim, second_rim):
        return ((first_rim.astype(jnp.float32) + second_rim.astype(jnp.float32)) * 0.5).astype(
            jnp.bfloat16
        )[:, None]

    top_row = jnp.concatenate(
        [
            corner(north_rim[:, 0], west_rim[:, 0]),
            north_rim,
            corner(north_rim[:, -1], east_rim[:, 0]),
        ],
        axis=1,
    )
    bottom_row = jnp.concatenate(
        [
            corner(south_rim[:, 0], west_rim[:, -1]),
            south_rim,
            corner(south_rim[:, -1], east_rim[:, -1]),
        ],
        axis=1,
    )
    middle = jnp.concatenate([west_rim[:, :, None], field_grid, east_rim[:, :, None]], axis=2)
    return jnp.concatenate([top_row[:, None], middle, bottom_row[:, None]], axis=1)


def flatten_weights(weights):
    return jnp.transpose(weights, (2, 0, 1, 3)).reshape(weights.shape[2], 9 * weights.shape[3])


def convolve(padded, weight_matrix):
    channels = padded.shape[0]
    side_len = padded.shape[1] - 2
    block_rows = math.gcd(side_len, 16)

    def conv_block(row_start):
        row_slab = lax.dynamic_slice_in_dim(padded, row_start, block_rows + 2, 1)
        windows = [
            row_slab[:, vertical : vertical + block_rows, lateral : lateral + side_len]
            for vertical in range(3)
            for lateral in range(3)
        ]
        patches = jnp.stack(windows).reshape(9 * channels, block_rows * side_len)
        return jnp.dot(weight_matrix, patches, preferred_element_type=jnp.float32)

    starts = jnp.arange(side_len // block_rows, dtype=jnp.int32) * block_rows
    blocks = lax.map(conv_block, starts)
    return jnp.transpose(blocks, (1, 0, 2)).reshape(weight_matrix.shape[0], side_len * side_len)


def extend(field_grid, seam, position):
    rim_edges = jnp.stack(
        [field_grid[:, 0, :], field_grid[:, :, -1], field_grid[:, -1, :], field_grid[:, :, 0]]
    )
    vectors = []
    for direction, step_by in ((0, TILE_ROW), (1, -1), (2, -TILE_ROW), (3, 1)):
        arrived = from_behind(rim_edges, "tile", step_by)
        vector = orient(arrived, seam[position, direction])
        vectors.append(vector)
    return assemble(field_grid, *vectors)


def shards(
    source,
    request_rows,
    cell_slots,
    cell_counts,
    seam,
    conv_first,
    bias_first,
    conv_second,
    bias_second,
):
    position = lax.axis_index("tile")
    halves = lax.axis_size("ch")
    core_index = lax.axis_index("ch")
    requests = request_rows[0]
    source_rows = lax.all_gather(source, "ch", axis=0, tiled=True)
    picked = jnp.take(
        source_rows,
        lax.all_to_all(requests, "tile", split_axis=0, concat_axis=0, tiled=True),
        axis=1,
    )
    fetched = lax.all_to_all(picked, "tile", split_axis=1, concat_axis=1, tiled=True)
    fetched = fetched.reshape(fetched.shape[0], fetched.shape[1] * fetched.shape[2])
    remapped = remap_cells(fetched, cell_slots[0], cell_counts[0])
    field_grid = remapped.reshape(remapped.shape[0], SIDE, SIDE)
    padded = extend(field_grid, seam, position)
    activated = jax.nn.gelu(
        convolve(padded, flatten_weights(conv_first)) + bias_first[:, None], approximate=True
    )
    hidden = activated.astype(jnp.bfloat16)
    hidden_padded = extend(hidden.reshape(hidden.shape[0], SIDE, SIDE), seam, position)
    out_share = remapped.shape[0] // halves
    out_start = core_index * out_share
    second_bias = lax.dynamic_slice_in_dim(bias_second, out_start, out_share, 0)
    own_field = lax.dynamic_slice_in_dim(remapped, out_start, out_share, 0)
    local_hidden = hidden_padded.shape[0]
    weights_in = lax.dynamic_slice_in_dim(conv_second, core_index * local_hidden, local_hidden, 3)
    second_matrix = flatten_weights(weights_in)
    response = lax.psum_scatter(
        convolve(hidden_padded, second_matrix), "ch", scatter_dimension=0, tiled=True
    )
    result = (own_field.astype(jnp.float32) + (response + second_bias[:, None])).astype(
        jnp.bfloat16
    )
    return result[None]


def solution(mesh):
    in_specs = (
        P("ch", ("grp", "tile")),
        P("tile", None, None),
        P("tile", None, None),
        P("tile", None, None),
        P(),
        P(None, None, "ch", None),
        P("ch"),
        P(),
        P(),
    )
    out_specs = P(("grp", "tile"), "ch", None)
    return jax.shard_map(shards, mesh=mesh, in_specs=in_specs, out_specs=out_specs, check_vma=False)
```

profile of v0, /device:TPU:0, one launch (start us, length us, event | category | flops | bytes accessed | tf_op | source)
XLA Modules:
  0.0 434.6 jit_solution(15505995135332921230)
XLA Ops:
  6.5 1.6 all_to_all.13
  8.1 7.3 %all-to-all-start = ((s32[8,1,2048]{2,1,0:T(1,128)}), s32[8,1,2048]{2,1,0:T(1,128)S(1)}, u32[]{:S(2)}, u32[]{:S(2)}) async-start(s32[8,1,2048]{2,1,0:T(1,128)} %all_to_all.13), calls=%async_computation | async-start | bytes 131072 | tf_op jit(solution)/shard_map/all_to_all | solution.py:116
  16.1 6.2 %all-to-all-done = s32[8,1,2048]{2,1,0:T(1,128)S(1)} async-done(((s32[8,1,2048]{2,1,0:T(1,128)}), s32[8,1,2048]{2,1,0:T(1,128)S(1)}, u32[]{:S(2)}, u32[]{:S(2)}) %all-to-all-start) | async-done | bytes 65568 | tf_op jit(solution)/shard_map/all_to_all | solution.py:116
  22.4 5.8 %all-gather.2.cloned.1.call-done = bf16[64,8192]{1,0:T(8,128)(2,1)} async-done(((bf16[32,8192]{1,0:T(8,128)(2,1)}), bf16[64,8192]{1,0:T(8,128)(2,1)}) %all-gather.2.cloned.1.call-update) | async-done | bytes 1048592 | tf_op jit(solution)/shard_map/all_gather | solution.py:113
  28.2 2.0 copy.158
  30.3 57.8 %gather_fusion = bf16[16384,64]{1,0:T(8,128)(2,1)} fusion(bf16[64,8192]{0,1:T(8,128)(2,1)S(1)} %copy.158, s32[16384]{0:T(1024)S(1)} %broadcast_clamp_fusion), kind=kCustom, calls=%fused_computation.4 | custom fusion | bytes 4259840 | tf_op jit(solution)/shard_map/jit(_take)/gather | solution.py:114
  88.1 3.5 copy.159
  91.6 1.6 select_bitcast_fusion
  93.2 5.9 %all-to-all-start.1 = ((bf16[64,8,2048]{2,0,1:T(8,128)(2,1)}), bf16[64,8,2048]{2,0,1:T(8,128)(2,1)S(1)}, u32[]{:S(2)}, u32[]{:S(2)}) async-start(bf16[64,8,2048]{2,0,1:T(8,128)(2,1)} %select_bitcast_fusion), calls=%async_computation.1 | async-start | bytes 4194304 | tf_op jit(solution)/shard_map/all_to_all | solution.py:119
  99.4 48.4 %all-to-all-done.1 = bf16[64,8,2048]{2,0,1:T(8,128)(2,1)S(1)} async-done(((bf16[64,8,2048]{2,0,1:T(8,128)(2,1)}), bf16[64,8,2048]{2,0,1:T(8,128)(2,1)S(1)}, u32[]{:S(2)}, u32[]{:S(2)}) %all-to-all-start.1) | async-done | bytes 2097184 | tf_op jit(solution)/shard_map/all_to_all | solution.py:119
  147.8 3.1 copy.160
  150.9 13.8 %gather_fusion.1 = bf16[4096,64]{1,0:T(8,128)(2,1)S(1)} fusion(bf16[64,16384]{0,1:T(8,128)(2,1)} %bitcast.230, s32[4096]{0:T(1024)S(1)} %fusion.29), kind=kCustom, calls=%fused_computation.clone | custom fusion | bytes 1064960 | tf_op jit(solution)/shard_map/jit(_take)/gather | solution.py:24
  164.7 13.8 %gather_fusion.2 = bf16[4096,64]{1,0:T(8,128)(2,1)S(1)} fusion(bf16[64,16384]{0,1:T(8,128)(2,1)} %bitcast.231, s32[4096]{0:T(1024)S(1)} %fusion.30), kind=kCustom, calls=%fused_computation.1.clone | custom fusion | bytes 1064960 | tf_op jit(solution)/shard_map/jit(_take)/gather | solution.py:24
  178.4 17.1 %gather_fusion.3 = bf16[4096,64]{1,0:T(8,128)(2,1)} fusion(bf16[64,16384]{0,1:T(8,128)(2,1)} %bitcast.232, s32[4096]{0:T(1024)S(1)} %fusion.31), kind=kCustom, calls=%fused_computation.2.clone | custom fusion | bytes 1064960 | tf_op jit(solution)/shard_map/jit(_take)/gather | solution.py:24
  195.5 17.1 %gather_fusion.4 = bf16[4096,64]{1,0:T(8,128)(2,1)} fusion(bf16[64,16384]{0,1:T(8,128)(2,1)} %bitcast.233, s32[4096]{0:T(1024)S(1)} %fusion.32), kind=kCustom, calls=%fused_computation.3.clone | custom fusion | bytes 1064960 | tf_op jit(solution)/shard_map/jit(_take)/gather | solution.py:24
  212.6 7.6 %divide_convert_fusion = bf16[64,4096]{0,1:T(8,128)(2,1)S(1)} fusion(bf16[4096,64]{1,0:T(8,128)(2,1)} %gather_fusion.4, bf16[4096,64]{1,0:T(8,128)(2,1)} %gather_fusion.3, bf16[4096,64]{1,0:T(8,128)(2,1)S(1)} %gather_fusion.2, bf16[4096,64]{1,0:T(8,128)(2,1)S(1)} %gather_fusion.1, f32[4096]{0:T(1024)S(1)} %bitcast.266, f32[4096]{0:T(1024)S(1)} %bitcast.267, ...), kind=kLoop, calls=%fused_computation.56 | loop fusion | flops 4456448 | bytes 2719744 | tf_op jit(solution)/shard_map/convert_element_type | solution.py:27
  221.3 1.5 constant_dynamic-slice_fusion.8
  234.1 2.4 collective-permute-start.2
  236.5 1.6 copy.169
  238.7 4.7 %collective-permute-done.1 = bf16[4,64,64]{2,1,0:T(8,128)(2,1)S(1)} collective-permute-done((bf16[4,64,64]{2,1,0:T(8,128)(2,1)S(1)}, bf16[4,64,64]{2,1,0:T(8,128)(2,1)S(1)}, u32[]{:S(2)}, u32[]{:S(2)}) %collective-permute-start.1) | collective-permute-done | bytes 32800 | tf_op jit(solution)/shard_map/ppermute | solution.py:14
  243.8 2.6 copy.170
  246.4 2.6 copy.168
  249.0 3.3 pad_maximum_fusion
  253.5 65.7 %while.20 = (s32[]{:T(128)}, f32[4,64,1024]{2,1,0:T(8,128)}, s32[4]{0:T(128)}, bf16[64,66,66]{2,1,0:T(8,128)(2,1)S(1)}, bf16[64,576]{1,0:T(8,128)(2,1)}, /*index=5*/s32[]{:T(128)}, s32[]{:T(128)}, s32[]{:T(128)}, s32[]{}, s32[]{}) while((s32[]{:T(128)}, f32[4,64,1024]{2,1,0:T(8,128)}, s32[4]{0:T(128)}, bf16[64,66,66]{2,1,0:T(8,128)(2,1)S(1)}, ...), condition=%wide.region_1.3_spmd, body=%wide.region_0.0_spmd.sunk | while | flops 75497480 | bytes 7422719 | solution.py:82
  253.5 1.2 dynamic_slice.94
  264.5 3.5 reshape.161
  268.0 1.9 fusion.101
  269.9 1.2 dynamic_slice.94
  280.9 3.5 reshape.161
  284.4 2.0 fusion.101
  286.3 1.2 dynamic_slice.94
  297.3 3.5 reshape.161
  300.8 1.9 fusion.101
  302.8 1.2 dynamic_slice.94
  313.8 3.5 reshape.161
  317.2 1.9 fusion.101
  319.2 1.9 copy.176
  321.1 2.2 reshape.99
  323.3 2.4 fusion.27
  325.7 1.5 slice_reduce_fusion.1
  328.6 1.8 collective-permute-start.5
  330.6 1.9 collective-permute-done.3
  333.2 4.2 collective-permute-done.4
  337.6 2.6 copy.184
  340.2 2.6 copy.183
  342.9 3.3 pad_maximum_fusion.1
  347.4 65.7 %while.21 = (s32[]{:T(128)}, f32[4,64,1024]{2,1,0:T(8,128)}, s32[4]{0:T(128)}, bf16[64,66,66]{2,1,0:T(8,128)(2,1)S(1)}, bf16[64,576]{1,0:T(8,128)(2,1)}, /*index=5*/s32[]{:T(128)}, s32[]{:T(128)}, s32[]{:T(128)}, s32[]{}, s32[]{}) while((s32[]{:T(128)}, f32[4,64,1024]{2,1,0:T(8,128)}, s32[4]{0:T(128)}, bf16[64,66,66]{2,1,0:T(8,128)(2,1)S(1)}, ...), condition=%wide.region_3.5_spmd, body=%wide.region_2.4_spmd.sunk | while | flops 75497480 | bytes 7422719 | solution.py:82
  347.4 1.2 dynamic_slice.95
  358.3 3.5 reshape.162
  361.8 1.9 fusion.113
  363.8 1.2 dynamic_slice.95
  374.8 3.5 reshape.162
  378.3 2.0 fusion.113
  380.2 1.2 dynamic_slice.95
  391.2 3.5 reshape.162
  394.7 1.9 fusion.113
  407.6 3.5 reshape.162
  411.1 1.9 fusion.113
  413.1 1.8 copy.191
  414.9 1.6 copy.201
  416.6 5.8 %reduce-scatter.4.cloned.1.call-done = f32[32,4096]{1,0:T(8,128)} async-done(((f32[64,4096]{1,0:T(8,128)}), f32[32,4096]{1,0:T(8,128)}) %reduce-scatter.4.cloned.1.call-update) | async-done | bytes 524304
  422.5 1.6 copy.202
  424.1 1.4 fusion.28
  425.6 2.2 copy.192
  (168 shorter events, 71.5 us)
Async XLA Ops:
  6.5 321.0 %copy-start = (bf16[3,3,64,128]{3,2,1,0:T(8,128)(2,1)S(1)}, bf16[3,3,64,128]{3,2,1,0:T(8,128)(2,1)}, u32[]{:S(2)}) copy-start(bf16[3,3,64,128]{3,2,1,0:T(8,128)(2,1)} %param.22) | copy-start | bytes 442372
  8.1 14.2 %all-to-all-start = ((s32[8,1,2048]{2,1,0:T(1,128)}), s32[8,1,2048]{2,1,0:T(1,128)S(1)}, u32[]{:S(2)}, u32[]{:S(2)}) async-start(s32[8,1,2048]{2,1,0:T(1,128)} %all_to_all.13), calls=%async_computation | async-start | bytes 131072 | tf_op jit(solution)/shard_map/all_to_all | solution.py:116
  15.3 12.9 %all-gather.2.cloned.1.call-start = ((), (), s32[]{:S(2)}) async-start(), calls=%async_computation.3 | async-start | bytes 1572864 | tf_op jit(solution)/shard_map/all_gather | solution.py:113
  93.2 5.9 %copy-start.2 = (s32[1,4,4096]{2,1,0:T(4,128)S(1)}, s32[1,4,4096]{2,1,0:T(4,128)}, u32[]{:S(2)}) copy-start(s32[1,4,4096]{2,1,0:T(4,128)} %param.18) | copy-start | bytes 196612
  93.2 6.0 %copy-start.3 = (s32[1,4,4096]{2,1,0:T(4,128)S(1)}, s32[1,4,4096]{2,1,0:T(4,128)}, u32[]{:S(2)}) copy-start(s32[1,4,4096]{2,1,0:T(4,128)} %param.17) | copy-start | bytes 196612
  93.2 54.6 %all-to-all-start.1 = ((bf16[64,8,2048]{2,0,1:T(8,128)(2,1)}), bf16[64,8,2048]{2,0,1:T(8,128)(2,1)S(1)}, u32[]{:S(2)}, u32[]{:S(2)}) async-start(bf16[64,8,2048]{2,0,1:T(8,128)(2,1)} %select_bitcast_fusion), calls=%async_computation.1 | async-start | bytes 4194304 | tf_op jit(solution)/shard_map/all_to_all | solution.py:119
  99.0 323.4 %reduce-scatter.4.cloned.1.call-start = ((), (), s32[]{:S(2)}) async-start(), calls=%async_computation.4 | async-start | bytes 1572864
  212.6 20.5 %copy-start.1 = (bf16[3,3,64,64]{3,2,1,0:T(8,128)(2,1)S(1)}, bf16[3,3,64,64]{3,2,1,0:T(8,128)(2,1)}, u32[]{:S(2)}) copy-start(bf16[3,3,64,64]{3,2,1,0:T(8,128)(2,1)} %param.20) | copy-start | bytes 221188
  220.7 17.4 %collective-permute-start = (bf16[4,64,64]{2,1,0:T(8,128)(2,1)S(1)}, bf16[4,64,64]{2,1,0:T(8,128)(2,1)S(1)}, u32[]{:S(2)}, u32[]{:S(2)}) collective-permute-start(bf16[4,64,64]{2,1,0:T(8,128)(2,1)S(1)} %pad_maximum_fusion.2), channel_id=1, source_target_pairs={{0,8},{2,10},{4,12},{6,14},{8,0},{10,2},{12,4},{14,6},{1,9},{3,11}... | collective-permute-start | bytes 98312 | tf_op jit(solution)/shard_map/ppermute | solution.py:14
  234.1 4.3 collective-permute-start.2
  236.5 7.0 %collective-permute-start.1 = (bf16[4,64,64]{2,1,0:T(8,128)(2,1)S(1)}, bf16[4,64,64]{2,1,0:T(8,128)(2,1)S(1)}, u32[]{:S(2)}, u32[]{:S(2)}) collective-permute-start(bf16[4,64,64]{2,1,0:T(8,128)(2,1)S(1)} %pad_maximum_fusion.2), channel_id=1, source_target_pairs={{0,2},{2,4},{4,6},{6,8},{8,10},{10,12},{12,14},{14,0},{1,3},{3,5},... | collective-permute-start | bytes 98312 | tf_op jit(solution)/shard_map/ppermute | solution.py:14
  321.1 2.2 copy-start.4
  327.3 5.3 %collective-permute-start.3 = (bf16[4,64,64]{2,1,0:T(8,128)(2,1)S(1)}, bf16[4,64,64]{2,1,0:T(8,128)(2,1)S(1)}, u32[]{:S(2)}, u32[]{:S(2)}) collective-permute-start(bf16[4,64,64]{2,1,0:T(8,128)(2,1)S(1)} %pad_maximum_fusion.3), channel_id=1, source_target_pairs={{0,8},{2,10},{4,12},{6,14},{8,0},{10,2},{12,4},{14,6},{1,9},{3,11}... | collective-permute-start | bytes 98312 | tf_op jit(solution)/shard_map/ppermute | solution.py:14
  328.6 4.3 collective-permute-start.5
  330.4 7.0 %collective-permute-start.4 = (bf16[4,64,64]{2,1,0:T(8,128)(2,1)S(1)}, bf16[4,64,64]{2,1,0:T(8,128)(2,1)S(1)}, u32[]{:S(2)}, u32[]{:S(2)}) collective-permute-start(bf16[4,64,64]{2,1,0:T(8,128)(2,1)S(1)} %pad_maximum_fusion.3), channel_id=1, source_target_pairs={{0,2},{2,4},{4,6},{6,8},{8,10},{10,12},{12,14},{14,0},{1,3},{3,5},... | collective-permute-start | bytes 98312 | tf_op jit(solution)/shard_map/ppermute | solution.py:14
  414.9 1.6 copy-start.5
Sparse Core Ops, SparseCore 0:
  17.7 10.4 all-gather.1
  416.7 5.7 reduce-scatter.3
where the time goes:
time: 437 us; the launch traced here: 435 us
  local copies, waits for them, and re-layouts  261 us (60%)
  waiting for transfers between devices  78.1 us (18%)
  between operations  24.3 us (6%)
  other arithmetic  20.6 us (5%)
  starting transfers between devices  18 us (4%)
  loops' own time  16.7 us (4%)
  matrix products  15.6 us (4%)
    gather x4, local copies, waits for them, and re-layouts, remap_cells(): picked = jnp.take(fetched, slot_table[entry], axis=1).astype(jnp.float32)  61.7 us
    gather x2, local copies, waits for them, and re-layouts, shards(): jnp.take(source_rows, lax.all_to_all(requests, 'tile', split_axis=0, conc...  61.3 us
    while x64, local copies, waits for them, and re-layouts  54.4 us
    all_to_all x1, waiting for transfers between devices, shards(): lax.all_to_all(picked, 'tile', split_axis=1, concat_axis=1, tiled=True)  48.4 us
    reshape x8, local copies, waits for them, and re-layouts, conv_block(): patches = jnp.stack(windows).reshape(9 * channels, block_rows * side_len)  27.9 us
    another operation x2, loops' own time, convolve(): blocks = lax.map(conv_block, starts)  16.7 us
    dot_general x8, matrix products, conv_block(): return jnp.dot(weight_matrix, patches, preferred_element_type=jnp.float32)  15.6 us
    ppermute x6, waiting for transfers between devices, from_behind(): return lax.ppermute(x, axis, [(i, (i + by) % size) for i in range(size)])  11.2 us
  transfers between devices with their start and end apart: 10, of which 9 were waited for; matrix products, arithmetic and copies ran while one was open for 2% of the time, Pallas kernels for 0%

commit v1 on v0

v1 whole, which is shorter than its diff:
```python
import functools

import jax
import jax.numpy as jnp
from jax import lax
from jax.experimental import pallas as pl
from jax.experimental.pallas import tpu as pltpu
from jax.sharding import PartitionSpec as P

SIDE = 64
TILE_ROW = 4
LANES = 128
MOVES = (TILE_ROW, -1, -TILE_ROW, 1)
BF = jnp.bfloat16
F32 = jnp.float32
SMEM = pl.BlockSpec(memory_space=pltpu.SMEM)
VMEM = pl.BlockSpec(memory_space=pltpu.VMEM)


def swap_core(x):
    return lax.ppermute(x, "ch", [(0, 1), (1, 0)])


def from_behind(x, by):
    size = lax.axis_size("tile")
    return lax.ppermute(x, "tile", [(i, (i + by) % size) for i in range(size)])


def pick_kernel(chunk, first_ref, second_ref, table_ref, out_ref, rows_ref):
    low = lax.broadcasted_iota(jnp.int32, (1, LANES), 1) < SIDE
    total = out_ref.shape[0]

    def step(block, carry):
        base = block * chunk

        def group(g, inner):
            for u in range(8):
                at = g * 8 + u
                left = table_ref[pl.ds(first_ref[base + at], 1), :]
                right = table_ref[pl.ds(second_ref[base + at], 1), :]
                rows_ref[pl.ds(at, 1), :] = jnp.where(low, left, right)
            return inner

        lax.fori_loop(0, chunk // 8, group, 0)
        out_ref[pl.ds(pl.multiple_of(base, chunk), chunk), :] = rows_ref[...].astype(BF)
        return carry

    lax.fori_loop(0, total // chunk, step, 0)


def pick_rows(first, second, table):
    total = first.shape[0]
    chunk = 128
    return pl.pallas_call(
        functools.partial(pick_kernel, chunk),
        out_shape=jax.ShapeDtypeStruct((total, LANES), BF),
        in_specs=[SMEM, SMEM, VMEM],
        out_specs=VMEM,
        scratch_shapes=[pltpu.VMEM((chunk, LANES), F32)],
        compiler_params=pltpu.CompilerParams(vmem_limit_bytes=32 * 2**20),
        name="pick_rows",
    )(first, second, table)


def remap_kernel(chunk, slots_ref, counts_ref, low_ref, high_ref, out_ref, table_ref, rows_ref):
    part = low_ref.shape[0]

    def fill(block, carry):
        at = pl.multiple_of(block * 128, 128)
        for which, ref in enumerate((low_ref, high_ref)):
            piece = ref[pl.ds(at, 128), :].astype(F32)
            table_ref[pl.ds(which * part + at, 128), :] = piece
            table_ref[pl.ds((2 + which) * part + at, 128), :] = pltpu.roll(piece, SIDE, 1)
        return carry

    lax.fori_loop(0, part // 128, fill, 0)
    entries = slots_ref.shape[0]
    cells = out_ref.shape[0]

    def step(block, carry):
        base = block * chunk

        def group(g, inner):
            for u in range(8):
                at = g * 8 + u
                for k in range(entries):
                    rows_ref[k, pl.ds(at, 1), :] = table_ref[pl.ds(slots_ref[k, base + at], 1), :]
            return inner

        lax.fori_loop(0, chunk // 8, group, 0)
        here = pl.ds(pl.multiple_of(base, chunk), chunk)
        weights = counts_ref[here, :]
        count = weights[:, 0:1]
        summed = weights[:, 0:1] * rows_ref[0]
        for k in range(1, entries):
            count = count + weights[:, k : k + 1]
            summed = summed + weights[:, k : k + 1] * rows_ref[k]
        out_ref[here, :] = (summed / count)[:, :SIDE].astype(BF)
        return carry

    lax.fori_loop(0, cells // chunk, step, 0)


def remap_cells(slots, counts, low, high):
    entries, cells = slots.shape
    chunk = 128
    return pl.pallas_call(
        functools.partial(remap_kernel, chunk),
        out_shape=jax.ShapeDtypeStruct((cells, SIDE), BF),
        in_specs=[SMEM, VMEM, VMEM, VMEM],
        out_specs=VMEM,
        scratch_shapes=[
            pltpu.VMEM((4 * low.shape[0], LANES), F32),
            pltpu.VMEM((entries, chunk, LANES), F32),
        ],
        compiler_params=pltpu.CompilerParams(vmem_limit_bytes=40 * 2**20),
        name="remap_cells",
    )(slots, counts, low, high)


def seam_choice(seam, position):
    tiles = seam.shape[0]
    place = jnp.arange(SIDE, dtype=jnp.int32)
    rows = []
    for side, by in enumerate(MOVES):
        code = lax.dynamic_index_in_dim(seam, (position + by) % tiles, 0, keepdims=False)[side]
        rows.append((code % 4) * SIDE + jnp.where(code >= 4, SIDE - 1 - place, place))
    wanted = jnp.concatenate(rows)
    return (wanted[:, None] == jnp.arange(4 * SIDE, dtype=jnp.int32)[None, :]).astype(BF)


def extend_half(half, choice, core):
    height = half.shape[0]
    pack = jnp.concatenate([half[0], half[-1], half[:, 0], half[:, -1]])
    other = swap_core(pack)
    upper = jnp.where(core == 0, pack, other)
    lower = jnp.where(core == 0, other, pack)
    a, b = 2 * SIDE, 2 * SIDE + height
    edges = jnp.concatenate([upper[:SIDE], upper[b:], lower[b:], lower[SIDE:a], upper[a:b], lower[a:b]])
    chosen = jnp.dot(choice, edges, preferred_element_type=F32).astype(BF)
    north, east, south, west = [
        from_behind(chosen[d * SIDE : (d + 1) * SIDE], by) for d, by in enumerate(MOVES)
    ]

    def corner(one, two):
        return ((one.astype(F32) + two.astype(F32)) * 0.5).astype(BF)[None]

    is_upper = core == 0
    above = jnp.where(is_upper, north, upper[SIDE:a])
    below = jnp.where(is_upper, lower[:SIDE], south)

    def column(rim, place):
        first = jnp.concatenate([corner(north[place], rim[0]), rim[: height + 1]])
        second = jnp.concatenate([rim[height - 1 :], corner(south[place], rim[-1])])
        return jnp.where(is_upper, first, second)[:, None]

    middle = jnp.concatenate([above[None], half, below[None]])
    return jnp.concatenate([column(west, 0), middle, column(east, SIDE - 1)], axis=1)


def convolve(padded, kernel):
    return lax.conv_general_dilated(
        padded[None],
        kernel,
        (1, 1),
        "VALID",
        dimension_numbers=("NHWC", "HWIO", "NHWC"),
        preferred_element_type=F32,
    )[0]


def shards(source, request_rows, cell_slots, cell_counts, seam, conv_first, bias_first, conv_second, bias_second):
    position = lax.axis_index("tile")
    core = lax.axis_index("ch")
    tiles, slots_each = request_rows.shape[1], request_rows.shape[2]
    share = slots_each // 2
    quarter = share // 2
    cells_half = cell_slots.shape[2] // 2

    requests = lax.dynamic_slice_in_dim(request_rows[0], core * share, share, 1)
    wanted = lax.all_to_all(requests, "tile", split_axis=0, concat_axis=0, tiled=True)
    sibling = swap_core(source)
    rows = jnp.where(
        core == 0, jnp.concatenate([source, sibling]), jnp.concatenate([sibling, source])
    ).T.astype(F32)
    table = jnp.concatenate([rows, rows], axis=1)
    wanted = wanted.reshape(tiles, 2, quarter)
    picked = pick_rows(wanted[:, 0].reshape(-1), wanted[:, 1].reshape(-1), table)
    arrived = lax.all_to_all(
        picked.reshape(tiles, quarter, LANES), "tile", split_axis=0, concat_axis=0, tiled=True
    ).reshape(tiles * quarter, LANES)
    across = swap_core(arrived)
    low = jnp.where(core == 0, arrived, across)
    high = jnp.where(core == 0, across, arrived)

    slots = lax.dynamic_slice_in_dim(cell_slots[0], core * cells_half, cells_half, 1)
    counts = lax.dynamic_slice_in_dim(cell_counts[0], core * cells_half, cells_half, 1)
    owner, place = slots // slots_each, slots % slots_each
    served, inside = place // share, place % share
    part = tiles * quarter
    table_rows = (inside // quarter) * (2 * part) + served * part + owner * quarter + inside % quarter
    remapped = remap_cells(table_rows, counts.astype(F32).T, low, high)

    choice = seam_choice(seam, position)
    first_kernel = jnp.transpose(lax.all_gather(conv_first, "ch", axis=2, tiled=True), (0, 1, 3, 2))
    first_bias = lax.all_gather(bias_first, "ch", axis=0, tiled=True)
    height = cells_half // SIDE
    grid = remapped.reshape(height, SIDE, SIDE)
    activated = jax.nn.gelu(convolve(extend_half(grid, choice, core), first_kernel) + first_bias, approximate=True)
    hidden = activated.astype(BF)
    second_kernel = jnp.transpose(conv_second, (0, 1, 3, 2))
    response = convolve(extend_half(hidden, choice, core), second_kernel) + bias_second
    result = (grid.astype(F32) + response).astype(BF).reshape(cells_half, SIDE).T
    mine = SIDE // 2
    kept = lax.dynamic_slice_in_dim(result, core * mine, mine, 0)
    sent = swap_core(lax.dynamic_slice_in_dim(result, (1 - core) * mine, mine, 0))
    return jnp.where(
        core == 0, jnp.concatenate([kept, sent], axis=1), jnp.concatenate([sent, kept], axis=1)
    )[None]


def solution(mesh):
    in_specs = (
        P("ch", ("grp", "tile")),
        P("tile", None, None),
        P("tile", None, None),
        P("tile", None, None),
        P(),
        P(None, None, "ch", None),
        P("ch"),
        P(),
        P(),
    )
    out_specs = P(("grp", "tile"), "ch", None)
    return jax.shard_map(shards, mesh=mesh, in_specs=in_specs, out_specs=out_specs, check_vma=False)
```

time: 437 us -> 130 us (0.30)
  local copies, waits for them, and re-layouts: 261 us -> 11.9 us
  waiting for transfers between devices: 78.1 us -> 31.4 us
  Pallas kernels: 0 us -> 31 us
  loops' own time: 16.7 us -> 0 us
  between operations: 24.3 us -> 11.8 us
  other arithmetic: 20.6 us -> 8.35 us
  matrix products: 15.6 us -> 3.53 us
  starting transfers between devices: 18 us -> 26.6 us
  blocking collectives: 0 us -> 4.46 us
    gather x6 -> x0, local copies, waits for them, and re-layouts: 123 us -> none  [the longest x4 61.7 us: remap_cells(): picked = jnp.take(fetched, slot_table[entry], axis=1).astype(jnp.float32)]
    while x66 -> x0, local copies, waits for them, and re-layouts: 55.9 us -> none
    all_to_all x1, waiting for transfers between devices: 48.4 us -> 12.3 us  [shards(): lax.all_to_all(picked.reshape(tiles, quarter, LANES), 'tile', split_axis=...]
    reshape x10 -> x2, local copies, waits for them, and re-layouts: 31.7 us -> 0.38 us  [the longest x1 0.34 us: shards(): grid = remapped.reshape(height, SIDE, SIDE)]
    pallas_call x0 -> x2, Pallas kernels: none -> 31 us  [the longest x1 19.9 us: remap_cells(): pl.pallas_call(functools.partial(remap_kernel, chunk), out_shape=jax.Shap...]
    another operation x2 -> x0, loops' own time: 16.7 us -> none  [convolve(): blocks = lax.map(conv_block, starts)]
    dot_general x8 -> x2, matrix products: 15.6 us -> 0.46 us  [extend_half(): chosen = jnp.dot(choice, edges, preferred_element_type=F32).astype(BF)]
    broadcast_in_dim x9 -> x6, local copies, waits for them, and re-layouts: 13 us -> 0.32 us  [the longest x2 0.21 us: convolve(): padded[None]]
  transfers between devices with their start and end apart: 10 -> 15, of which waited for: 9 -> 8; matrix products, arithmetic and copies ran while one was open for 2% -> 5% of each run, Pallas kernels for 0% -> 0%
where the time goes in v1:
time: 130 us; the launch traced here: 129 us
  waiting for transfers between devices  31.4 us (24%)
  Pallas kernels  31 us (24%)
  starting transfers between devices  26.6 us (20%)
  local copies, waits for them, and re-layouts  11.9 us (9%)
  between operations  11.8 us (9%)
  other arithmetic  8.35 us (6%)
  blocking collectives  4.46 us (3%)
  matrix products  3.53 us (3%)
    pallas_call x1, Pallas kernels, remap_cells(): pl.pallas_call(functools.partial(remap_kernel, chunk), out_shape=jax.Shap...  19.9 us
    ppermute x8, starting transfers between devices, from_behind(): return lax.ppermute(x, 'tile', [(i, (i + by) % size) for i in range(size)])  15.3 us
    all_to_all x1, waiting for transfers between devices, shards(): lax.all_to_all(picked.reshape(tiles, quarter, LANES), 'tile', split_axis=...  12.3 us
    pallas_call x1, Pallas kernels, pick_rows(): pl.pallas_call(functools.partial(pick_kernel, chunk), out_shape=jax.Shape...  11.1 us
    ppermute x8, waiting for transfers between devices, from_behind(): return lax.ppermute(x, 'tile', [(i, (i + by) % size) for i in range(size)])  8.09 us
    all_to_all x1, starting transfers between devices, shards(): lax.all_to_all(requests, 'tile', split_axis=0, concat_axis=0, tiled=True)  6.85 us
    ppermute x5, waiting for transfers between devices, swap_core(): return lax.ppermute(x, 'ch', [(0, 1), (1, 0)])  6.28 us
    all_to_all x1, waiting for transfers between devices, shards(): lax.all_to_all(requests, 'tile', split_axis=0, concat_axis=0, tiled=True)  4.75 us
  transfers between devices with their start and end apart: 15, of which 8 were waited for; matrix products, arithmetic and copies ran while one was open for 5% of the time, Pallas kernels for 0%

profile of v1, /device:TPU:0, one launch (start us, length us, event | category | flops | bytes accessed | tf_op | source)
XLA Modules:
  0.0 129.1 jit_solution(4450387754318019047)
XLA Ops:
  0.0 0.5 collective-permute-start
  0.5 0.8 constant_dynamic-slice_fusion.4
  1.2 0.6 all_to_all.9
  1.9 6.9 %all-to-all-start = ((s32[8,1,1024]{2,1,0:T(1,128)}), s32[8,1,1024]{2,1,0:T(1,128)S(1)}, u32[]{:S(2)}, u32[]{:S(2)}) async-start(s32[8,1,1024]{2,1,0:T(1,128)} %all_to_all.9), calls=%async_computation | async-start | bytes 65536 | tf_op jit(solution)/shard_map/all_to_all | solution.py:181
  8.7 1.9 %copy.61 = bf16[32,8192]{0,1:T(8,128)(2,1)S(1)} copy(bf16[32,8192]{1,0:T(8,128)(2,1)} %param.9) | data formatting | bytes 1048576 | tf_op args[0]
  10.6 4.7 %all-to-all-done = s32[8,1,1024]{2,1,0:T(1,128)S(1)} async-done(((s32[8,1,1024]{2,1,0:T(1,128)}), s32[8,1,1024]{2,1,0:T(1,128)S(1)}, u32[]{:S(2)}, u32[]{:S(2)}) %all-to-all-start) | async-done | bytes 32800 | tf_op jit(solution)/shard_map/all_to_all | solution.py:181
  15.4 0.1 reduce
  15.6 1.8 %copy.62 = bf16[32,8192]{0,1:T(8,128)(2,1)} copy(bf16[32,8192]{1,0:T(8,128)(2,1)S(1)} %collective-permute-done) | data formatting | bytes 1048576 | tf_op jit(solution)/shard_map/ppermute | solution.py:21
  17.3 4.5 %fusion = bf16[8192,64]{1,0:T(8,128)(2,1)S(1)} fusion(bf16[32,8192]{0,1:T(8,128)(2,1)} %copy.62, bf16[32,8192]{0,1:T(8,128)(2,1)S(1)} %copy.61, pred[]{:T(512)S(6)} %eq.38), kind=kLoop, calls=%fused_computation.1 | loop fusion | flops 4718592 | bytes 2097153 | tf_op jit(solution)/shard_map/convert_element_type | solution.py:185
  21.8 1.0 maximum_convert_fusion.table_ref
  22.9 11.1 %pick_rows.1 = bf16[4096,128]{1,0:T(8,128)(2,1)} custom-call(s32[4096]{0:T(1024)S(1)} %bitcast.143, s32[4096]{0:T(1024)S(1)} %bitcast.142, f32[8192,128]{1,0:T(8,128)S(1)} %maximum_convert_fusion.table_ref), custom_call_target="tpu_custom_call" | custom-call | tf_op jit(solution)/shard_map/pick_rows/pallas_call | solution.py:54
  34.0 3.7 %all-to-all-start.1 = ((bf16[8,512,128]{2,1,0:T(8,128)(2,1)}), bf16[8,512,128]{2,1,0:T(8,128)(2,1)S(1)}, u32[]{:S(2)}, u32[]{:S(2)}) async-start(bf16[8,512,128]{2,1,0:T(8,128)(2,1)} %bitcast.6), calls=%async_computation.1 | async-start | bytes 2097152 | tf_op jit(solution)/shard_map/all_to_all | solution.py:189
  37.8 0.1 constant_dynamic-slice_fusion.3
  37.9 0.5 slice.194
  41.0 0.5 slice.195
  44.1 0.5 slice.196
  47.2 0.5 slice.197
  50.4 0.4 copy.95
  50.8 12.3 %all-to-all-done.1 = bf16[8,512,128]{2,1,0:T(8,128)(2,1)S(1)} async-done(((bf16[8,512,128]{2,1,0:T(8,128)(2,1)}), bf16[8,512,128]{2,1,0:T(8,128)(2,1)S(1)}, u32[]{:S(2)}, u32[]{:S(2)}) %all-to-all-start.1) | async-done | bytes 1048608 | tf_op jit(solution)/shard_map/all_to_all | solution.py:189
  63.1 0.2 fusion.33.slots_ref
  63.3 0.1 convert_bitcast_fusion.counts_ref
  63.4 2.3 %collective-permute-done.1 = bf16[4096,128]{1,0:T(8,128)(2,1)S(1)} collective-permute-done((bf16[4096,128]{1,0:T(8,128)(2,1)S(1)}, bf16[4096,128]{1,0:T(8,128)(2,1)S(1)}, u32[]{:S(2)}, u32[]{:S(2)}) %collective-permute-start.1) | collective-permute-done | bytes 1048608 | tf_op jit(solution)/shard_map/ppermute | solution.py:21
  65.7 0.2 broadcast_select_fusion
  65.9 19.9 %remap_cells.1 = bf16[2048,64]{1,0:T(8,128)(2,1)S(1)} custom-call(s32[4,2048]{1,0:T(4,128)S(1)} %fusion.33.slots_ref, f32[2048,4]{1,0:T(8,128)S(1)} %convert_bitcast_fusion.counts_ref, bf16[4096,128]{1,0:T(8,128)(2,1)S(1)} %get-tuple-element.6.low_ref, bf16[4096,128]{1,0:T(8,128)(2,1)S(1)} %get-tuple-element.5.high_ref), custom_call_target="tpu_custom_call" | custom-call | tf_op jit(solution)/shard_map/remap_cells/pallas_call | solution.py:107
  85.9 0.3 copy.65
  86.2 0.2 collective-permute-start.2
  86.4 0.1 pad_add_fusion
  86.5 1.0 collective-permute-done.2
  87.6 0.2 convolution_convert_fusion.1
  87.9 0.1 collective-permute-start.3
  88.0 2.0 %all_gather.6 = bf16[3,3,128,64]{3,2,1,0:T(8,128)(2,1)S(1)} all-gather(bf16[3,3,64,64]{3,2,1,0:T(8,128)(2,1)S(1)} %copy-done.1), channel_id=1, replica_groups=mesh['grp'=2,'tile'=8,'ch'=2] {'ch'}, dimensions={2}, use_global_device_ids=true | all-gather | bytes 221184 | tf_op jit(solution)/shard_map/all_gather | solution.py:205
  90.0 0.6 dynamic-slice.11
  91.2 0.2 dynamic-update-slice
  91.5 2.4 %all-reduce = f32[128]{0:T(128)S(1)} all-reduce(f32[128]{0:T(128)S(1)} %dynamic-update-slice), channel_id=1, replica_groups=mesh['grp'=2,'tile'=8,'ch'=2] {'ch'}, use_global_device_ids=true, to_apply=%add | all-reduce | flops 128 | bytes 1024
  93.9 2.9 %collective-permute-start.5 = (bf16[64,64]{1,0:T(8,128)(2,1)S(1)}, bf16[64,64]{1,0:T(8,128)(2,1)S(1)}, u32[]{:S(2)}, u32[]{:S(2)}) collective-permute-start(bf16[64,64]{1,0:T(8,128)(2,1)S(1)} %get-tuple-element.27), channel_id=1, source_target_pairs={{0,8},{2,10},{4,12},{6,14},{8,0},{10,2},{12,4},{14,6},{1,9},{3,11}... | collective-permute-start | bytes 24584 | tf_op jit(solution)/shard_map/ppermute | solution.py:26
  96.8 1.2 collective-permute-start.4
  98.1 3.5 %collective-permute-start.6 = (bf16[64,64]{1,0:T(8,128)(2,1)S(1)}, bf16[64,64]{1,0:T(8,128)(2,1)S(1)}, u32[]{:S(2)}, u32[]{:S(2)}) collective-permute-start(bf16[64,64]{1,0:T(8,128)(2,1)S(1)} %get-tuple-element.26), channel_id=1, source_target_pairs={{0,14},{2,0},{4,2},{6,4},{8,6},{10,8},{12,10},{14,12},{1,15},{3,1}... | collective-permute-start | bytes 24584 | tf_op jit(solution)/shard_map/ppermute | solution.py:26
  101.6 1.7 %collective-permute-done.4 = bf16[64,64]{1,0:T(8,128)(2,1)S(1)} collective-permute-done((bf16[64,64]{1,0:T(8,128)(2,1)S(1)}, bf16[64,64]{1,0:T(8,128)(2,1)S(1)}, u32[]{:S(2)}, u32[]{:S(2)}) %collective-permute-start.4) | collective-permute-done | bytes 8224 | tf_op jit(solution)/shard_map/ppermute | solution.py:26
  103.4 0.3 maximum_bitcast_fusion
  103.8 0.1 pad
  103.9 0.1 copy.76
  104.0 0.4 copy-done.8
  104.4 1.5 %convolution_select_fusion.1 = f32[32,8,9,128]{3,1,2,0:T(8,128)S(1)} fusion(bf16[3,3,128,64]{3,2,1,0:T(8,128)(2,1)S(1)} %all_gather.6, bf16[34,1,7,2,64]{4,2,3,0,1:T(8,128)(2,1)S(1)} %slice.288, bf16[34,1,8,9,64]{4,2,3,0,1:T(8,128)(2,1)S(1)} %copy.76, pred[8,9]{0,1:T(8,128)(4,1)S(1)} %copy-done.8), kind=kOutput, calls=%fused_computation.9 | convolution fusion | flops 341182464 | bytes 1701448 | tf_op jit(solution)/shard_map/conv_general_dilated | solution.py:162
  106.0 0.2 copy.77
  106.2 0.4 fusion.10
  106.7 0.1 collective-permute-start.7
  106.8 1.2 collective-permute-done.7
  108.1 0.2 convolution_convert_fusion
  108.4 0.1 collective-permute-start.8
  108.5 2.9 %collective-permute-start.10 = (bf16[64,128]{1,0:T(8,128)(2,1)S(1)}, bf16[64,128]{1,0:T(8,128)(2,1)S(1)}, u32[]{:S(2)}, u32[]{:S(2)}) collective-permute-start(bf16[64,128]{1,0:T(8,128)(2,1)S(1)} %get-tuple-element.23), channel_id=1, source_target_pairs={{0,8},{2,10},{4,12},{6,14},{8,0},{10,2},{12,4},{14,6},{1,9},{3,11}... | collective-permute-start | bytes 49160 | tf_op jit(solution)/shard_map/ppermute | solution.py:26
  111.4 4.6 %collective-permute-start.11 = (bf16[64,128]{1,0:T(8,128)(2,1)S(1)}, bf16[64,128]{1,0:T(8,128)(2,1)S(1)}, u32[]{:S(2)}, u32[]{:S(2)}) collective-permute-start(bf16[64,128]{1,0:T(8,128)(2,1)S(1)} %get-tuple-element.22), channel_id=1, source_target_pairs={{0,14},{2,0},{4,2},{6,4},{8,6},{10,8},{12,10},{14,12},{1,15},{3,1}... | collective-permute-start | bytes 49160 | tf_op jit(solution)/shard_map/ppermute | solution.py:26
  116.0 6.4 %collective-permute-done.9 = bf16[64,128]{1,0:T(8,128)(2,1)S(1)} collective-permute-done((bf16[64,128]{1,0:T(8,128)(2,1)S(1)}, bf16[64,128]{1,0:T(8,128)(2,1)S(1)}, u32[]{:S(2)}, u32[]{:S(2)}) %collective-permute-start.9) | collective-permute-done | bytes 16416 | tf_op jit(solution)/shard_map/ppermute | solution.py:26
  122.6 0.4 maximum_bitcast_fusion.1
  123.0 0.1 copy.85
  123.2 1.5 %convolution_select_fusion = f32[32,8,9,64]{3,1,2,0:T(8,128)S(1)} fusion(bf16[3,3,64,128]{3,2,1,0:T(8,128)(2,1)S(1)} %copy-done, bf16[34,1,7,2,128]{4,2,3,0,1:T(8,128)(2,1)S(1)} %slice.318, bf16[34,1,8,9,128]{4,2,3,0,1:T(8,128)(2,1)S(1)} %copy.85, pred[8,9]{0,1:T(8,128)(4,1)S(1)} %copy-done.8), kind=kOutput, calls=%fused_computation.8 | convolution fusion | flops 342183936 | bytes 1485896 | tf_op jit(solution)/shard_map/conv_general_dilated | solution.py:162
  124.7 0.2 copy.86
  125.0 0.6 copy.87
  125.7 0.1 fusion.13
  125.8 0.4 dynamic-slice_bitcast_fusion.1
  126.2 0.1 collective-permute-start.12
  126.3 0.2 copy.88
  126.5 1.7 %collective-permute-done.12 = bf16[32,2048]{0,1:T(8,128)(2,1)S(1)} collective-permute-done((bf16[32,2048]{0,1:T(8,128)(2,1)S(1)}, bf16[32,2048]{0,1:T(8,128)(2,1)S(1)}, u32[]{:S(2)}, u32[]{:S(2)}) %collective-permute-start.12) | collective-permute-done | bytes 131104 | tf_op jit(solution)/shard_map/ppermute | solution.py:21
  128.2 0.2 copy.89
  128.4 0.8 maximum_select_fusion.1
  (79 shorter events, 0.9 us)
Async XLA Ops:
  0.0 123.2 %copy-start = (bf16[3,3,64,128]{3,2,1,0:T(8,128)(2,1)S(1)}, bf16[3,3,64,128]{3,2,1,0:T(8,128)(2,1)}, u32[]{:S(2)}) copy-start(bf16[3,3,64,128]{3,2,1,0:T(8,128)(2,1)} %param.16) | copy-start | bytes 442372
  0.0 15.5 %collective-permute-start = (bf16[32,8192]{1,0:T(8,128)(2,1)}, bf16[32,8192]{1,0:T(8,128)(2,1)S(1)}, u32[]{:S(2)}, u32[]{:S(2)}) collective-permute-start(bf16[32,8192]{1,0:T(8,128)(2,1)} %param.9), channel_id=1, source_target_pairs={{0,1},{1,0},{2,3},{3,2},{4,5},{5,4},{6,7},{7,6},{8,9},{9,8},{10,11... | collective-permute-start | bytes 1572872 | tf_op jit(solution)/shard_map/ppermute | solution.py:21
  1.9 13.5 %all-to-all-start = ((s32[8,1,1024]{2,1,0:T(1,128)}), s32[8,1,1024]{2,1,0:T(1,128)S(1)}, u32[]{:S(2)}, u32[]{:S(2)}) async-start(s32[8,1,1024]{2,1,0:T(1,128)} %all_to_all.9), calls=%async_computation | async-start | bytes 65536 | tf_op jit(solution)/shard_map/all_to_all | solution.py:181
  34.0 3.8 %copy-start.2 = (s32[8,4]{0,1:T(4,128)S(1)}, s32[8,4]{0,1:T(4,128)}, u32[]{:S(2)}) copy-start(s32[8,4]{0,1:T(4,128)} %param.13) | copy-start | bytes 388
  34.0 16.3 %copy-start.3 = (s32[1,4,4096]{2,1,0:T(4,128)S(1)}, s32[1,4,4096]{2,1,0:T(4,128)}, u32[]{:S(2)}) copy-start(s32[1,4,4096]{2,1,0:T(4,128)} %param.12) | copy-start | bytes 196612
  34.0 29.1 %copy-start.4 = (s32[1,4,4096]{2,1,0:T(4,128)S(1)}, s32[1,4,4096]{2,1,0:T(4,128)}, u32[]{:S(2)}) copy-start(s32[1,4,4096]{2,1,0:T(4,128)} %param.11) | copy-start | bytes 196612
  34.0 29.0 %all-to-all-start.1 = ((bf16[8,512,128]{2,1,0:T(8,128)(2,1)}), bf16[8,512,128]{2,1,0:T(8,128)(2,1)S(1)}, u32[]{:S(2)}, u32[]{:S(2)}) async-start(bf16[8,512,128]{2,1,0:T(8,128)(2,1)} %bitcast.6), calls=%async_computation.1 | async-start | bytes 2097152 | tf_op jit(solution)/shard_map/all_to_all | solution.py:189
  63.1 2.7 %collective-permute-start.1 = (bf16[4096,128]{1,0:T(8,128)(2,1)S(1)}, bf16[4096,128]{1,0:T(8,128)(2,1)S(1)}, u32[]{:S(2)}, u32[]{:S(2)}) collective-permute-start(bf16[4096,128]{1,0:T(8,128)(2,1)S(1)} %bitcast.146), channel_id=1, source_target_pairs={{0,1},{1,0},{2,3},{3,2},{4,5},{5,4},{6,7},{7,6},{8,9},{9,8},{10,11... | collective-permute-start | bytes 3145736 | tf_op jit(solution)/shard_map/ppermute | solution.py:21
  85.8 2.2 %copy-start.1 = (bf16[3,3,64,64]{3,2,1,0:T(8,128)(2,1)S(1)}, bf16[3,3,64,64]{3,2,1,0:T(8,128)(2,1)}, u32[]{:S(2)}) copy-start(bf16[3,3,64,64]{3,2,1,0:T(8,128)(2,1)} %param.14) | copy-start | bytes 221188
  85.8 4.2 %copy-start.7 = (u32[32]{0:T(128)S(1)}, u32[32]{0:T(128)}, u32[]{:S(2)}) copy-start(u32[32]{0:T(128)} %constant.177) | copy-start | bytes 388
  85.8 5.4 %copy-start.6 = (f32[64]{0:T(128)S(1)}, f32[64]{0:T(128)}, u32[]{:S(2)}) copy-start(f32[64]{0:T(128)} %param.15) | copy-start | bytes 772
  86.2 1.3 %collective-permute-start.2 = (bf16[192,64]{1,0:T(8,128)(2,1)S(1)}, bf16[192,64]{1,0:T(8,128)(2,1)S(1)}, u32[]{:S(2)}, u32[]{:S(2)}) collective-permute-start(bf16[192,64]{1,0:T(8,128)(2,1)S(1)} %pad_maximum_fusion), channel_id=1, source_target_pairs={{0,1},{1,0},{2,3},{3,2},{4,5},{5,4},{6,7},{7,6},{8,9},{9,8},{10,11... | collective-permute-start | bytes 73736 | tf_op jit(solution)/shard_map/ppermute | solution.py:21
  87.9 13.7 %collective-permute-start.3 = (bf16[64,64]{1,0:T(8,128)(2,1)S(1)}, bf16[64,64]{1,0:T(8,128)(2,1)S(1)}, u32[]{:S(2)}, u32[]{:S(2)}) collective-permute-start(bf16[64,64]{1,0:T(8,128)(2,1)S(1)} %get-tuple-element.28), channel_id=1, source_target_pairs={{0,8},{2,10},{4,12},{6,14},{8,0},{10,2},{12,4},{14,6},{1,9},{3,11}... | collective-permute-start | bytes 24584 | tf_op jit(solution)/shard_map/ppermute | solution.py:26
  93.9 7.6 %collective-permute-start.5 = (bf16[64,64]{1,0:T(8,128)(2,1)S(1)}, bf16[64,64]{1,0:T(8,128)(2,1)S(1)}, u32[]{:S(2)}, u32[]{:S(2)}) collective-permute-start(bf16[64,64]{1,0:T(8,128)(2,1)S(1)} %get-tuple-element.27), channel_id=1, source_target_pairs={{0,8},{2,10},{4,12},{6,14},{8,0},{10,2},{12,4},{14,6},{1,9},{3,11}... | collective-permute-start | bytes 24584 | tf_op jit(solution)/shard_map/ppermute | solution.py:26
  96.8 6.4 %collective-permute-start.4 = (bf16[64,64]{1,0:T(8,128)(2,1)S(1)}, bf16[64,64]{1,0:T(8,128)(2,1)S(1)}, u32[]{:S(2)}, u32[]{:S(2)}) collective-permute-start(bf16[64,64]{1,0:T(8,128)(2,1)S(1)} %get-tuple-element.25), channel_id=1, source_target_pairs={{0,2},{2,4},{4,6},{6,8},{8,10},{10,12},{12,14},{14,0},{1,3},{3,5},... | collective-permute-start | bytes 24584 | tf_op jit(solution)/shard_map/ppermute | solution.py:26
  98.1 5.3 %collective-permute-start.6 = (bf16[64,64]{1,0:T(8,128)(2,1)S(1)}, bf16[64,64]{1,0:T(8,128)(2,1)S(1)}, u32[]{:S(2)}, u32[]{:S(2)}) collective-permute-start(bf16[64,64]{1,0:T(8,128)(2,1)S(1)} %get-tuple-element.26), channel_id=1, source_target_pairs={{0,14},{2,0},{4,2},{6,4},{8,6},{10,8},{12,10},{14,12},{1,15},{3,1}... | collective-permute-start | bytes 24584 | tf_op jit(solution)/shard_map/ppermute | solution.py:26
  103.7 0.7 copy-start.8
  106.7 1.3 %collective-permute-start.7 = (bf16[192,128]{1,0:T(8,128)(2,1)S(1)}, bf16[192,128]{1,0:T(8,128)(2,1)S(1)}, u32[]{:S(2)}, u32[]{:S(2)}) collective-permute-start(bf16[192,128]{1,0:T(8,128)(2,1)S(1)} %pad_maximum_fusion.1), channel_id=1, source_target_pairs={{0,1},{1,0},{2,3},{3,2},{4,5},{5,4},{6,7},{7,6},{8,9},{9,8},{10,11... | collective-permute-start | bytes 147464 | tf_op jit(solution)/shard_map/ppermute | solution.py:21
  108.4 7.6 %collective-permute-start.8 = (bf16[64,128]{1,0:T(8,128)(2,1)S(1)}, bf16[64,128]{1,0:T(8,128)(2,1)S(1)}, u32[]{:S(2)}, u32[]{:S(2)}) collective-permute-start(bf16[64,128]{1,0:T(8,128)(2,1)S(1)} %get-tuple-element.24), channel_id=1, source_target_pairs={{0,8},{2,10},{4,12},{6,14},{8,0},{10,2},{12,4},{14,6},{1,9},{3,11}... | collective-permute-start | bytes 49160 | tf_op jit(solution)/shard_map/ppermute | solution.py:26
  108.5 7.6 %collective-permute-start.10 = (bf16[64,128]{1,0:T(8,128)(2,1)S(1)}, bf16[64,128]{1,0:T(8,128)(2,1)S(1)}, u32[]{:S(2)}, u32[]{:S(2)}) collective-permute-start(bf16[64,128]{1,0:T(8,128)(2,1)S(1)} %get-tuple-element.23), channel_id=1, source_target_pairs={{0,8},{2,10},{4,12},{6,14},{8,0},{10,2},{12,4},{14,6},{1,9},{3,11}... | collective-permute-start | bytes 49160 | tf_op jit(solution)/shard_map/ppermute | solution.py:26
  111.4 11.1 %collective-permute-start.11 = (bf16[64,128]{1,0:T(8,128)(2,1)S(1)}, bf16[64,128]{1,0:T(8,128)(2,1)S(1)}, u32[]{:S(2)}, u32[]{:S(2)}) collective-permute-start(bf16[64,128]{1,0:T(8,128)(2,1)S(1)} %get-tuple-element.22), channel_id=1, source_target_pairs={{0,14},{2,0},{4,2},{6,4},{8,6},{10,8},{12,10},{14,12},{1,15},{3,1}... | collective-permute-start | bytes 49160 | tf_op jit(solution)/shard_map/ppermute | solution.py:26
  116.0 6.4 %collective-permute-start.9 = (bf16[64,128]{1,0:T(8,128)(2,1)S(1)}, bf16[64,128]{1,0:T(8,128)(2,1)S(1)}, u32[]{:S(2)}, u32[]{:S(2)}) collective-permute-start(bf16[64,128]{1,0:T(8,128)(2,1)S(1)} %get-tuple-element.21), channel_id=1, source_target_pairs={{0,2},{2,4},{4,6},{6,8},{8,10},{10,12},{12,14},{14,0},{1,3},{3,5},... | collective-permute-start | bytes 49160 | tf_op jit(solution)/shard_map/ppermute | solution.py:26
  125.0 0.7 copy-start.5
  126.2 2.0 %collective-permute-start.12 = (bf16[32,2048]{0,1:T(8,128)(2,1)S(1)}, bf16[32,2048]{0,1:T(8,128)(2,1)S(1)}, u32[]{:S(2)}, u32[]{:S(2)}) collective-permute-start(bf16[32,2048]{0,1:T(8,128)(2,1)S(1)} %get-tuple-element.8), channel_id=1, source_target_pairs={{0,1},{1,0},{2,3},{3,2},{4,5},{5,4},{6,7},{7,6},{8,9},{9,8},{10,11... | collective-permute-start | bytes 393224 | tf_op jit(solution)/shard_map/ppermute | solution.py:21

commit v2 on v1

--- a/solution.py
+++ b/solution.py
@@ -118,55 +118,212 @@
     )(slots, counts, low, high)
 
 
-def seam_choice(seam, position):
+def seam_choice(seam, position, core, height):
     tiles = seam.shape[0]
     place = jnp.arange(SIDE, dtype=jnp.int32)
     rows = []
     for side, by in enumerate(MOVES):
         code = lax.dynamic_index_in_dim(seam, (position + by) % tiles, 0, keepdims=False)[side]
-        rows.append((code % 4) * SIDE + jnp.where(code >= 4, SIDE - 1 - place, place))
+        edge = code % 4
+        cell = jnp.where(code >= 4, SIDE - 1 - place, place)
+        near = cell - core * height
+        column = jnp.where((near >= 0) & (near < height), 2 * SIDE + jnp.where(edge == 1, height, 0) + near, -1)
+        row = jnp.where(core == edge // 2, core * SIDE + cell, -1)
+        rows.append(jnp.where(edge % 2 == 0, row, column))
     wanted = jnp.concatenate(rows)
-    return (wanted[:, None] == jnp.arange(4 * SIDE, dtype=jnp.int32)[None, :]).astype(BF)
-
-
-def extend_half(half, choice, core):
-    height = half.shape[0]
-    pack = jnp.concatenate([half[0], half[-1], half[:, 0], half[:, -1]])
-    other = swap_core(pack)
-    upper = jnp.where(core == 0, pack, other)
-    lower = jnp.where(core == 0, other, pack)
-    a, b = 2 * SIDE, 2 * SIDE + height
-    edges = jnp.concatenate([upper[:SIDE], upper[b:], lower[b:], lower[SIDE:a], upper[a:b], lower[a:b]])
-    chosen = jnp.dot(choice, edges, preferred_element_type=F32).astype(BF)
-    north, east, south, west = [
-        from_behind(chosen[d * SIDE : (d + 1) * SIDE], by) for d, by in enumerate(MOVES)
+    width = 2 * SIDE + 2 * height
+    return (wanted[:, None] == jnp.arange(width, dtype=jnp.int32)[None, :]).astype(BF)
+
+
+def block_kernel(
+    half_ref, choice_ref, first_ref, first_bias_ref, second_ref, second_bias_ref, out_ref,
+    field, hidden, west_buf, east_buf, left_shift, right_shift, mid_buf, pack_one, pack_two,
+    send_one, send_two, recv_one, recv_two, halo_one, halo_two, other_first, other_bias,
+    first_full, turned, send_sems, recv_sems, side_sems,
+):
+    grp, tile, core = (lax.axis_index(name) for name in ("grp", "tile", "ch"))
+    tiles = lax.axis_size("tile")
+    sibling = (grp, tile, 1 - core)
+    upper = core == 0
+    cells = half_ref.shape[0]
+    height = cells // SIDE
+    rows = cells + 2 * SIDE
+    start = 8
+    body = start + SIDE
+    targets = [lax.rem(tile + by + tiles, tiles) for by in MOVES]
+    sources = [lax.rem(tile - by + tiles, tiles) for by in MOVES]
+
+    barrier = pltpu.get_barrier_semaphore()
+    pl.semaphore_signal(barrier, inc=1, device_id=sibling, device_id_type=pl.DeviceIdType.MESH)
+    for other in targets:
+        for c in range(2):
+            pl.semaphore_signal(barrier, inc=1, device_id=(grp, other, c), device_id_type=pl.DeviceIdType.MESH)
+
+    field[pl.ds(body, cells), :] = half_ref[...].astype(F32)
+    pl.semaphore_wait(barrier, 9)
+
+    def remote(src, dst, send_sem, recv_sem, device):
+        return pltpu.make_async_remote_copy(
+            src_ref=src, dst_ref=dst, send_sem=send_sem, recv_sem=recv_sem,
+            device_id=device, device_id_type=pl.DeviceIdType.MESH,
+        )
+
+    def begin(rnd, grid, pack, send, recv, halo):
+        pack[0:SIDE, :] = grid[body : body + SIDE, :].astype(BF)
+        pack[SIDE : 2 * SIDE, :] = grid[body + cells - SIDE : body + cells, :].astype(BF)
+        a = 2 * SIDE
+        pack[a : a + height, :] = grid[pl.ds(body, height, stride=SIDE), :].astype(BF)
+        pack[a + height : a + 2 * height, :] = grid[pl.ds(body + SIDE - 1, height, stride=SIDE), :].astype(BF)
+        rims = jnp.dot(choice_ref[...], pack[...], preferred_element_type=F32).astype(BF)
+        for d in range(4):
+            send[d] = rims[d * SIDE : (d + 1) * SIDE]
+        copies = []
+        for d in range(4):
+            for c in range(2):
+                copies.append(
+                    remote(
+                        send.at[d], recv.at[core, d], send_sems.at[rnd, 2 * d + c],
+                        recv_sems.at[rnd, core * 4 + d], (grp, targets[d], c),
+                    )
+                )
+        inner = pl.multiple_of((1 - core) * SIDE, SIDE)
+        copies.append(
+            remote(pack.at[pl.ds(inner, SIDE), :], halo, send_sems.at[rnd, 8], recv_sems.at[rnd, 8], sibling)
+        )
+        for copy in copies:
+            copy.start()
+        return copies
+
+    def finish(rnd, copies, grid, send, recv, halo, left, right, mid, width):
+        lanes = slice(0, width)
+        for d in range(4):
+            for c in range(2):
+                remote(
+                    send.at[d], recv.at[c, d], send_sems.at[rnd, 2 * d + c],
+                    recv_sems.at[rnd, c * 4 + d], (grp, sources[d], c),
+                ).wait_recv()
+        copies[-1].wait_recv()
+        north, east, south, west = [recv[0, d].astype(F32) + recv[1, d].astype(F32) for d in range(4)]
+        inside = halo[...].astype(F32)
+        grid[start:body, :] = jnp.where(upper, north, inside)
+        grid[body + cells : body + cells + SIDE, :] = jnp.where(upper, inside, south)
+
+        def corner(one, two):
+            return ((one + two) * 0.5).astype(BF).astype(F32)
+
+        def column(buf, rim, place):
+            buf[8 : 8 + SIDE, lanes] = rim
+            buf[7:8, lanes] = corner(north[place : place + 1], rim[0:1])
+            buf[8 + SIDE : 9 + SIDE, lanes] = corner(south[place : place + 1], rim[SIDE - 1 : SIDE])
+            return jnp.where(
+                upper, buf[7 : 9 + height, lanes], buf[7 + SIDE - height : 9 + SIDE, lanes]
+            )
+
+        west_cells = column(west_buf, west, 0)
+        east_cells = column(east_buf, east, SIDE - 1)
+        left[...] = grid[start - 1 : start - 1 + rows, :]
+        left[pl.ds(0, height + 2, stride=SIDE), :] = west_cells
+        right[...] = grid[start + 1 : start + 1 + rows, :]
+        right[pl.ds(SIDE - 1, height + 2, stride=SIDE), :] = east_cells
+        mid[0, :, lanes] = left[...].astype(BF)
+        mid[1, :, lanes] = grid[start : start + rows, :].astype(BF)
+        mid[2, :, lanes] = right[...].astype(BF)
+        for copy in copies:
+            copy.wait_send()
+
+    block = 256
+
+    def convolve(mid, weights, at, width):
+        total = None
+        for a in range(3):
+            for b in range(3):
+                piece = mid[b, pl.ds(pl.multiple_of(at + a * SIDE, SIDE), block), 0:width]
+                term = jnp.dot(piece, weights[3 * a + b], preferred_element_type=F32)
+                total = term if total is None else total + term
+        return total
+
+    weight_copy = remote(first_ref, other_first, side_sems.at[0], side_sems.at[1], sibling)
+    bias_copy = remote(first_bias_ref, other_bias, side_sems.at[2], side_sems.at[3], sibling)
+    copies = begin(0, field, pack_one, send_one, recv_one, halo_one)
+    weight_copy.start()
+    bias_copy.start()
+    weight_copy.wait()
+    bias_copy.wait()
+    mine, other = first_ref[...], other_first[...]
+    first_full[:, :, 0:SIDE] = jnp.where(upper, mine, other)
+    first_full[:, :, SIDE:] = jnp.where(upper, other, mine)
+    mine, other = first_bias_ref[0:1, :], other_bias[0:1, :]
+    bias = jnp.concatenate([jnp.where(upper, mine, other), jnp.where(upper, other, mine)], axis=1)
+    finish(0, copies, field, send_one, recv_one, halo_one, left_shift[0], right_shift[0], mid_buf, SIDE)
+
+    def first(step, carry):
+        at = pl.multiple_of(step * block, block)
+        v = convolve(mid_buf, first_full, at, SIDE) + bias
+        act = 0.5 * v * (1.0 + jnp.tanh(0.7978845608028654 * (v + 0.044715 * (v * v * v))))
+        hidden[pl.ds(pl.multiple_of(body + at, 8), block), :] = act.astype(BF).astype(F32)
+        return carry
+
+    lax.fori_loop(0, cells // block, first, 0)
+    copies = begin(1, hidden, pack_two, send_two, recv_two, halo_two)
+    finish(1, copies, hidden, send_two, recv_two, halo_two, left_shift[1], right_shift[1], mid_buf, 2 * SIDE)
+
+    def second(step, carry):
+        at = pl.multiple_of(step * block, block)
+        v = convolve(mid_buf, second_ref, at, 2 * SIDE) + second_bias_ref[...]
+        v = v + field[pl.ds(pl.multiple_of(body + at, 8), block), :]
+        turned[:, pl.ds(at, block)] = v.T.astype(BF)
+        return carry
+
+    lax.fori_loop(0, cells // block, second, 0)
+    share = SIDE // 2
+    away = remote(
+        turned.at[pl.ds(pl.multiple_of((1 - core) * share, share), share), :],
+        out_ref.at[:, pl.ds(pl.multiple_of(core * cells, cells), cells)],
+        side_sems.at[4], side_sems.at[5], sibling,
+    )
+    away.start()
+    out_ref[:, pl.ds(pl.multiple_of(core * cells, cells), cells)] = turned[
+        pl.ds(pl.multiple_of(core * share, share), share), :
     ]
-
-    def corner(one, two):
-        return ((one.astype(F32) + two.astype(F32)) * 0.5).astype(BF)[None]
-
-    is_upper = core == 0
-    above = jnp.where(is_upper, north, upper[SIDE:a])
-    below = jnp.where(is_upper, lower[:SIDE], south)
-
-    def column(rim, place):
-        first = jnp.concatenate([corner(north[place], rim[0]), rim[: height + 1]])
-        second = jnp.concatenate([rim[height - 1 :], corner(south[place], rim[-1])])
-        return jnp.where(is_upper, first, second)[:, None]
-
-    middle = jnp.concatenate([above[None], half, below[None]])
-    return jnp.concatenate([column(west, 0), middle, column(east, SIDE - 1)], axis=1)
-
-
-def convolve(padded, kernel):
-    return lax.conv_general_dilated(
-        padded[None],
+    away.wait()
+
+
+def conv_block(half, choice, first, first_bias, second, second_bias):
+    cells, chans = half.shape
+    hid = 2 * chans
+    rows = cells + 2 * SIDE
+    pack = choice.shape[1]
+    shape = pltpu.VMEM
+
+    def kernel(*refs):
+        ins, rest = refs[:7], list(refs[7:])
+        l1, l2, r1, r2 = rest[4:8]
+        block_kernel(*ins, *rest[:4], (l1, l2), (r1, r2), *rest[8:])
+
+    return pl.pallas_call(
         kernel,
-        (1, 1),
-        "VALID",
-        dimension_numbers=("NHWC", "HWIO", "NHWC"),
-        preferred_element_type=F32,
-    )[0]
+        out_shape=jax.ShapeDtypeStruct((chans // 2, 2 * cells), BF),
+        in_specs=[VMEM] * 6,
+        out_specs=VMEM,
+        scratch_shapes=[
+            shape((rows + 16, chans), F32), shape((rows + 16, hid), F32),
+            shape((SIDE + 16, hid), F32), shape((SIDE + 16, hid), F32),
+            shape((rows, chans), F32), shape((rows, hid), F32),
+            shape((rows, chans), F32), shape((rows, hid), F32),
+            shape((3, rows, hid), BF),
+            shape((pack, chans), BF), shape((pack, hid), BF),
+            shape((4, SIDE, chans), BF), shape((4, SIDE, hid), BF),
+            shape((2, 4, SIDE, chans), BF), shape((2, 4, SIDE, hid), BF),
+            shape((SIDE, chans), BF), shape((SIDE, hid), BF),
+            shape(first.shape, BF), shape(first_bias.shape, F32),
+            shape((9, chans, hid), BF), shape((chans, cells), BF),
+            pltpu.SemaphoreType.DMA((2, 9)), pltpu.SemaphoreType.DMA((2, 9)), pltpu.SemaphoreType.DMA((6,)),
+        ],
+        compiler_params=pltpu.CompilerParams(
+            collective_id=0, has_side_effects=True, vmem_limit_bytes=48 * 2**20
+        ),
+        name="conv_block",
+    )(half, choice, first, first_bias, second, second_bias)
 
 
 def shards(source, request_rows, cell_slots, cell_counts, seam, conv_first, bias_first, conv_second, bias_second):
@@ -201,21 +358,14 @@
     table_rows = (inside // quarter) * (2 * part) + served * part + owner * quarter + inside % quarter
     remapped = remap_cells(table_rows, counts.astype(F32).T, low, high)
 
-    choice = seam_choice(seam, position)
-    first_kernel = jnp.transpose(lax.all_gather(conv_first, "ch", axis=2, tiled=True), (0, 1, 3, 2))
-    first_bias = lax.all_gather(bias_first, "ch", axis=0, tiled=True)
-    height = cells_half // SIDE
-    grid = remapped.reshape(height, SIDE, SIDE)
-    activated = jax.nn.gelu(convolve(extend_half(grid, choice, core), first_kernel) + first_bias, approximate=True)
-    hidden = activated.astype(BF)
-    second_kernel = jnp.transpose(conv_second, (0, 1, 3, 2))
-    response = convolve(extend_half(hidden, choice, core), second_kernel) + bias_second
-    result = (grid.astype(F32) + response).astype(BF).reshape(cells_half, SIDE).T
-    mine = SIDE // 2
-    kept = lax.dynamic_slice_in_dim(result, core * mine, mine, 0)
-    sent = swap_core(lax.dynamic_slice_in_dim(result, (1 - core) * mine, mine, 0))
-    return jnp.where(
-        core == 0, jnp.concatenate([kept, sent], axis=1), jnp.concatenate([sent, kept], axis=1)
+    choice = seam_choice(seam, position, core, cells_half // SIDE)
+
+    def arrange(weights):
+        return jnp.transpose(weights, (0, 1, 3, 2)).reshape(9, weights.shape[3], weights.shape[2])
+
+    bias_rows = jnp.broadcast_to(bias_first[None], (8, bias_first.shape[0]))
+    return conv_block(
+        remapped, choice, arrange(conv_first), bias_rows, arrange(conv_second), bias_second[None]
     )[None]
 
 

time: 130 us -> 108 us (0.83)
  Pallas kernels: 31 us -> 52.1 us
  starting transfers between devices: 26.6 us -> 11.4 us
  waiting for transfers between devices: 31.4 us -> 18.1 us
  blocking collectives: 4.46 us -> 0 us
  matrix products: 3.53 us -> 0 us
  local copies, waits for them, and re-layouts: 11.9 us -> 8.42 us
  other arithmetic: 8.35 us -> 6.28 us
    pallas_call x0 -> x1, Pallas kernels: none -> 21.1 us  [conv_block(): pl.pallas_call(kernel, out_shape=jax.ShapeDtypeStruct((chans // 2, 2 * ce...]
    ppermute x8 -> x0, starting transfers between devices: 15.3 us -> none  [from_behind(): return lax.ppermute(x, 'tile', [(i, (i + by) % size) for i in range(size)])]
    ppermute x8 -> x0, waiting for transfers between devices: 8.09 us -> none  [from_behind(): return lax.ppermute(x, 'tile', [(i, (i + by) % size) for i in range(size)])]
    ppermute x5 -> x2, waiting for transfers between devices: 6.28 us -> 2.21 us  [swap_core(): return lax.ppermute(x, 'ch', [(0, 1), (1, 0)])]
    conv_general_dilated x2 -> x0, matrix products: 3.08 us -> none  [convolve(): lax.conv_general_dilated(padded[None], kernel, (1, 1), 'VALID', dimension...]
    unnamed x1 -> x0, blocking collectives: 2.44 us -> none
    all_gather x1 -> x0, blocking collectives: 2.02 us -> none  [shards(): lax.all_gather(conv_first, 'ch', axis=2, tiled=True)]
    conv_general_dilated x8 -> x0, local copies, waits for them, and re-layouts: 1.39 us -> none  [convolve(): lax.conv_general_dilated(padded[None], kernel, (1, 1), 'VALID', dimension...]
  transfers between devices with their start and end apart: 15 -> 4, of which waited for: 8 -> 3; matrix products, arithmetic and copies ran while one was open for 5% -> 5% of each run, Pallas kernels for 0% -> 0%
where the time goes in v2:
time: 108 us; the launch traced here: 107 us
  Pallas kernels  52.1 us (48%)
  waiting for transfers between devices  18.1 us (17%)
  starting transfers between devices  11.4 us (11%)
  between operations  10.7 us (10%)
  local copies, waits for them, and re-layouts  8.42 us (8%)
  other arithmetic  6.28 us (6%)
    pallas_call x1, Pallas kernels, conv_block(): pl.pallas_call(kernel, out_shape=jax.ShapeDtypeStruct((chans // 2, 2 * ce...  21.1 us
    pallas_call x1, Pallas kernels, remap_cells(): pl.pallas_call(functools.partial(remap_kernel, chunk), out_shape=jax.Shap...  19.9 us
    all_to_all x1, waiting for transfers between devices, shards(): lax.all_to_all(picked.reshape(tiles, quarter, LANES), 'tile', split_axis=...  11.2 us
    pallas_call x1, Pallas kernels, pick_rows(): pl.pallas_call(functools.partial(pick_kernel, chunk), out_shape=jax.Shape...  11.1 us
    all_to_all x1, starting transfers between devices, shards(): lax.all_to_all(requests, 'tile', split_axis=0, concat_axis=0, tiled=True)  7.25 us
    all_to_all x1, waiting for transfers between devices, shards(): lax.all_to_all(requests, 'tile', split_axis=0, concat_axis=0, tiled=True)  4.75 us
    convert_element_type x1, other arithmetic, shards(): rows = jnp.where(core == 0, jnp.concatenate([source, sibling]), jnp.conca...  4.52 us
    all_to_all x1, starting transfers between devices, shards(): lax.all_to_all(picked.reshape(tiles, quarter, LANES), 'tile', split_axis=...  3.7 us
  transfers between devices with their start and end apart: 4, of which 3 were waited for; matrix products, arithmetic and copies ran while one was open for 5% of the time, Pallas kernels for 0%

profile of v2, /device:TPU:0, one launch (start us, length us, event | category | flops | bytes accessed | tf_op | source)
XLA Modules:
  0.0 107.1 jit_solution(2335972287860820540)
XLA Ops:
  0.0 0.0 copy-start
  0.0 0.5 collective-permute-start
  0.5 0.4 copy-done
  0.8 0.6 all_to_all.9
  1.5 7.3 %all-to-all-start = ((s32[8,1,1024]{2,1,0:T(1,128)}), s32[8,1,1024]{2,1,0:T(1,128)S(1)}, u32[]{:S(2)}, u32[]{:S(2)}) async-start(s32[8,1,1024]{2,1,0:T(1,128)} %all_to_all.9), calls=%async_computation | async-start | bytes 65536 | tf_op jit(solution)/shard_map/all_to_all | solution.py:338
  8.7 1.9 %copy.17 = bf16[32,8192]{0,1:T(8,128)(2,1)S(1)} copy(bf16[32,8192]{1,0:T(8,128)(2,1)} %param.9) | data formatting | bytes 1048576 | tf_op args[0]
  10.7 4.7 %all-to-all-done = s32[8,1,1024]{2,1,0:T(1,128)S(1)} async-done(((s32[8,1,1024]{2,1,0:T(1,128)}), s32[8,1,1024]{2,1,0:T(1,128)S(1)}, u32[]{:S(2)}, u32[]{:S(2)}) %all-to-all-start) | async-done | bytes 32800 | tf_op jit(solution)/shard_map/all_to_all | solution.py:338
  15.4 0.1 reduce
  15.6 0.0 collective-permute-done
  15.6 1.7 %copy.18 = bf16[32,8192]{0,1:T(8,128)(2,1)} copy(bf16[32,8192]{1,0:T(8,128)(2,1)S(1)} %collective-permute-done) | data formatting | bytes 1048576 | tf_op jit(solution)/shard_map/ppermute | solution.py:21
  17.3 4.5 %fusion = bf16[8192,64]{1,0:T(8,128)(2,1)S(1)} fusion(bf16[32,8192]{0,1:T(8,128)(2,1)} %copy.18, bf16[32,8192]{0,1:T(8,128)(2,1)S(1)} %copy.17, pred[]{:T(512)S(6)} %eq.71), kind=kLoop, calls=%fused_computation.1 | loop fusion | flops 4718592 | bytes 2097153 | tf_op jit(solution)/shard_map/convert_element_type | solution.py:342
  21.9 1.0 maximum_convert_fusion.table_ref
  22.9 11.1 %pick_rows.1 = bf16[4096,128]{1,0:T(8,128)(2,1)} custom-call(s32[4096]{0:T(1024)S(1)} %bitcast.42, s32[4096]{0:T(1024)S(1)} %bitcast.41, f32[8192,128]{1,0:T(8,128)S(1)} %maximum_convert_fusion.table_ref), custom_call_target="tpu_custom_call" | custom-call | tf_op jit(solution)/shard_map/pick_rows/pallas_call | solution.py:54
  34.0 0.0 copy-start.4
  34.0 0.0 copy-start.5
  34.0 0.0 copy-start.2
  34.0 0.0 copy-start.3
  34.0 0.0 copy-start.6
  34.0 3.7 %all-to-all-start.1 = ((bf16[8,512,128]{2,1,0:T(8,128)(2,1)}), bf16[8,512,128]{2,1,0:T(8,128)(2,1)S(1)}, u32[]{:S(2)}, u32[]{:S(2)}) async-start(bf16[8,512,128]{2,1,0:T(8,128)(2,1)} %bitcast.6), calls=%async_computation.1 | async-start | bytes 2097152 | tf_op jit(solution)/shard_map/all_to_all | solution.py:346
  37.8 0.0 copy-done.4
  37.8 0.1 constant_dynamic-slice_fusion.3
  37.9 0.5 slice.24
  40.3 0.5 slice.25
  44.1 0.5 slice.26
  46.5 0.5 slice.27
  50.5 0.0 copy-done.5
  50.5 0.4 copy.23
  50.8 0.0 copy-done.2
  50.9 0.2 copy.22
  51.1 0.0 copy-done.3
  51.1 0.2 copy.21
  51.3 11.2 %all-to-all-done.1 = bf16[8,512,128]{2,1,0:T(8,128)(2,1)S(1)} async-done(((bf16[8,512,128]{2,1,0:T(8,128)(2,1)}), bf16[8,512,128]{2,1,0:T(8,128)(2,1)S(1)}, u32[]{:S(2)}, u32[]{:S(2)}) %all-to-all-start.1) | async-done | bytes 1048608 | tf_op jit(solution)/shard_map/all_to_all | solution.py:346
  62.5 0.0 collective-permute-start.1
  62.5 0.1 pad_add_fusion
  62.6 0.0 copy-done.6
  62.6 0.2 fusion.5.slots_ref
  62.7 0.1 fusion.1.refs_1_
  62.9 0.1 convert_bitcast_fusion.counts_ref
  62.9 2.2 %collective-permute-done.1 = bf16[4096,128]{1,0:T(8,128)(2,1)S(1)} collective-permute-done((bf16[4096,128]{1,0:T(8,128)(2,1)S(1)}, bf16[4096,128]{1,0:T(8,128)(2,1)S(1)}, u32[]{:S(2)}, u32[]{:S(2)}) %collective-permute-start.1) | collective-permute-done | bytes 1048608 | tf_op jit(solution)/shard_map/ppermute | solution.py:21
  65.1 0.2 broadcast_select_fusion
  65.3 0.0 copy-start.7
  65.4 0.0 copy-start.1
  65.4 19.9 %remap_cells.1.refs_0_ = bf16[2048,64]{1,0:T(8,128)(2,1)S(1)} custom-call(s32[4,2048]{1,0:T(4,128)S(1)} %fusion.5.slots_ref, f32[2048,4]{1,0:T(8,128)S(1)} %convert_bitcast_fusion.counts_ref, bf16[4096,128]{1,0:T(8,128)(2,1)S(1)} %get-tuple-element.6.low_ref, bf16[4096,128]{1,0:T(8,128)(2,1)S(1)} %get-tuple-element.5.high_ref), custom_call_target="tpu_custom_call" | custom-call | tf_op jit(solution)/shard_map/remap_cells/pallas_call | solution.py:107
  85.2 0.0 copy-done.7
  85.3 0.0 copy-done.1
  85.3 21.1 %conv_block.1 = bf16[32,4096]{1,0:T(8,128)(2,1)S(1)} custom-call(bf16[2048,64]{1,0:T(8,128)(2,1)S(1)} %remap_cells.1.refs_0_, bf16[256,192]{1,0:T(8,128)(2,1)S(1)} %fusion.1.refs_1_, bf16[9,64,64]{2,1,0:T(8,128)(2,1)S(1)} %bitcast.40, f32[8,64]{1,0:T(8,128)S(1)} %broadcast_in_dim.27.refs_3_, bf16[9,128,64]{2,1,0:T(8,128)(2,1)S(1)} %bitcast.38, ...), custom_call_target="tpu_custom_call" | custom-call | tf_op jit(solution)/shard_map/conv_block/pallas_call | solution.py:303
  106.3 0.7 copy.25
  (7 shorter events, 0.1 us)
Async XLA Ops:
  0.0 0.8 copy-start
  0.0 15.6 %collective-permute-start = (bf16[32,8192]{1,0:T(8,128)(2,1)}, bf16[32,8192]{1,0:T(8,128)(2,1)S(1)}, u32[]{:S(2)}, u32[]{:S(2)}) collective-permute-start(bf16[32,8192]{1,0:T(8,128)(2,1)} %param.9), channel_id=1, source_target_pairs={{0,1},{1,0},{2,3},{3,2},{4,5},{5,4},{6,7},{7,6},{8,9},{9,8},{10,11... | collective-permute-start | bytes 1572872 | tf_op jit(solution)/shard_map/ppermute | solution.py:21
  1.5 13.9 %all-to-all-start = ((s32[8,1,1024]{2,1,0:T(1,128)}), s32[8,1,1024]{2,1,0:T(1,128)S(1)}, u32[]{:S(2)}, u32[]{:S(2)}) async-start(s32[8,1,1024]{2,1,0:T(1,128)} %all_to_all.9), calls=%async_computation | async-start | bytes 65536 | tf_op jit(solution)/shard_map/all_to_all | solution.py:338
  34.0 3.8 %copy-start.4 = (s32[8,4]{0,1:T(4,128)S(1)}, s32[8,4]{0,1:T(4,128)}, u32[]{:S(2)}) copy-start(s32[8,4]{0,1:T(4,128)} %param.13) | copy-start | bytes 388
  34.0 16.4 %copy-start.5 = (s32[1,4,4096]{2,1,0:T(4,128)S(1)}, s32[1,4,4096]{2,1,0:T(4,128)}, u32[]{:S(2)}) copy-start(s32[1,4,4096]{2,1,0:T(4,128)} %param.12) | copy-start | bytes 196612
  34.0 16.8 %copy-start.2 = (bf16[3,3,64,128]{3,2,1,0:T(8,128)(2,1)S(1)}, bf16[3,3,64,128]{3,2,1,0:T(8,128)(2,1)}, u32[]{:S(2)}) copy-start(bf16[3,3,64,128]{3,2,1,0:T(8,128)(2,1)} %param.16) | copy-start | bytes 442372
  34.0 17.1 %copy-start.3 = (bf16[3,3,64,64]{3,2,1,0:T(8,128)(2,1)S(1)}, bf16[3,3,64,64]{3,2,1,0:T(8,128)(2,1)}, u32[]{:S(2)}) copy-start(bf16[3,3,64,64]{3,2,1,0:T(8,128)(2,1)} %param.14) | copy-start | bytes 221188
  34.0 28.5 %copy-start.6 = (s32[1,4,4096]{2,1,0:T(4,128)S(1)}, s32[1,4,4096]{2,1,0:T(4,128)}, u32[]{:S(2)}) copy-start(s32[1,4,4096]{2,1,0:T(4,128)} %param.11) | copy-start | bytes 196612
  34.0 28.4 %all-to-all-start.1 = ((bf16[8,512,128]{2,1,0:T(8,128)(2,1)}), bf16[8,512,128]{2,1,0:T(8,128)(2,1)S(1)}, u32[]{:S(2)}, u32[]{:S(2)}) async-start(bf16[8,512,128]{2,1,0:T(8,128)(2,1)} %bitcast.6), calls=%async_computation.1 | async-start | bytes 2097152 | tf_op jit(solution)/shard_map/all_to_all | solution.py:346
  62.5 2.7 %collective-permute-start.1 = (bf16[4096,128]{1,0:T(8,128)(2,1)S(1)}, bf16[4096,128]{1,0:T(8,128)(2,1)S(1)}, u32[]{:S(2)}, u32[]{:S(2)}) collective-permute-start(bf16[4096,128]{1,0:T(8,128)(2,1)S(1)} %bitcast.44), channel_id=1, source_target_pairs={{0,1},{1,0},{2,3},{3,2},{4,5},{5,4},{6,7},{7,6},{8,9},{9,8},{10,11... | collective-permute-start | bytes 3145736 | tf_op jit(solution)/shard_map/ppermute | solution.py:21
  65.3 19.9 %copy-start.7 = (f32[64]{0:T(128)S(1)}, f32[64]{0:T(128)}, u32[]{:S(2)}) copy-start(f32[64]{0:T(128)} %param.15) | copy-start | bytes 772
  65.4 19.9 %copy-start.1 = (f32[64]{0:T(128)S(1)}, f32[64]{0:T(128)}, u32[]{:S(2)}) copy-start(f32[64]{0:T(128)} %param.17) | copy-start | bytes 772

commit v3 on v2

--- a/solution.py
+++ b/solution.py
@@ -17,74 +17,186 @@
 VMEM = pl.BlockSpec(memory_space=pltpu.VMEM)
 
 
-def swap_core(x):
-    return lax.ppermute(x, "ch", [(0, 1), (1, 0)])
-
-
-def from_behind(x, by):
-    size = lax.axis_size("tile")
-    return lax.ppermute(x, "tile", [(i, (i + by) % size) for i in range(size)])
-
-
-def pick_kernel(chunk, first_ref, second_ref, table_ref, out_ref, rows_ref):
+def fetch_kernel(
+    source_ref, wanted_ref, out_ref, other_source, asked, asked_here, table_ref, rows_ref, send_ref,
+    side_sems, ask_send, ask_recv, data_send, data_recv, pass_send, pass_recv,
+):
+    grp, tile, core = (lax.axis_index(name) for name in ("grp", "tile", "ch"))
+    tiles = lax.axis_size("tile")
+    mesh_id = pl.DeviceIdType.MESH
+    sibling = (grp, tile, 1 - core)
+    quarter = rows_ref.shape[0]
+
+    def offset(n):
+        return 1 + lax.rem(n + tiles // 2 - 1, tiles - 1)
+
+    barrier = pltpu.get_barrier_semaphore()
+    pl.semaphore_signal(barrier, inc=1, device_id=sibling, device_id_type=mesh_id)
+
+    def greet(n, carry):
+        other = lax.rem(tile + offset(n), tiles)
+        pl.semaphore_signal(barrier, inc=1, device_id=(grp, other, core), device_id_type=mesh_id)
+        return carry
+
+    lax.fori_loop(0, tiles - 1, greet, 0)
+    pl.semaphore_wait(barrier, tiles)
+
+    def remote(src, dst, send_sem, recv_sem, device):
+        return pltpu.make_async_remote_copy(
+            src_ref=src, dst_ref=dst, send_sem=send_sem, recv_sem=recv_sem,
+            device_id=device, device_id_type=mesh_id,
+        )
+
+    swap = remote(source_ref, other_source, side_sems.at[0], side_sems.at[1], sibling)
+    swap.start()
+
+    def ask_copy(owner, slot, sem_at):
+        return remote(
+            wanted_ref.at[owner], asked.at[slot], ask_send.at[owner], ask_recv.at[sem_at], (grp, owner, core)
+        )
+
+    def ask(n, carry):
+        owner = lax.rem(tile + offset(n), tiles)
+        ask_copy(owner, tile, tile).start()
+        return carry
+
+    lax.fori_loop(0, tiles - 1, ask, 0)
+    asked[tile] = wanted_ref[tile]
+
+    def answered(n, carry):
+        asker = lax.rem(tile + offset(n), tiles)
+        ask_copy(asker, asker, asker).wait_recv()
+        return carry
+
+    lax.fori_loop(0, tiles - 1, answered, 0)
+    to_scalars = pltpu.make_async_copy(asked, asked_here, side_sems.at[2])
+    to_scalars.start()
+    swap.wait()
+    upper = core == 0
+    chans = 2 * source_ref.shape[0]
+    cells = source_ref.shape[1]
+    span = 512
+    spread = (
+        lax.broadcasted_iota(jnp.int32, (chans, LANES), 1) % chans
+        == lax.broadcasted_iota(jnp.int32, (chans, LANES), 0)
+    ).astype(BF)
+
+    def fill(block, carry):
+        at = pl.ds(pl.multiple_of(block * span, span), span)
+        mine, other = source_ref[:, at].astype(F32), other_source[:, at].astype(F32)
+        both = jnp.concatenate([jnp.where(upper, mine, other), jnp.where(upper, other, mine)])
+        table_ref[at, :] = lax.dot_general(
+            both.astype(BF), spread, (((0,), (0,)), ((), ())), preferred_element_type=F32
+        )
+        return carry
+
+    lax.fori_loop(0, cells // span, fill, 0)
+    to_scalars.wait()
     low = lax.broadcasted_iota(jnp.int32, (1, LANES), 1) < SIDE
-    total = out_ref.shape[0]
+
+    def pick(who):
+        def group(g, inner):
+            base = g * 16
+            for u in range(16):
+                left = table_ref[pl.ds(asked_here[who, 0, base + u], 1), :]
+                right = table_ref[pl.ds(asked_here[who, 0, base + (quarter + u)], 1), :]
+                rows_ref[pl.ds(base + u, 1), :] = jnp.where(low, left, right)
+            return inner
+
+        lax.fori_loop(0, quarter // 16, group, 0)
+        return rows_ref[...].astype(BF)
+
+    def data_copy(to, slot, sem_at):
+        return remote(
+            send_ref.at[to], out_ref.at[core, slot], data_send.at[to], data_recv.at[sem_at], (grp, to, core)
+        )
+
+    def serve(n, carry):
+        asker = lax.rem(tile + offset(n), tiles)
+        send_ref[asker] = pick(asker)
+        data_copy(asker, tile, tile).start()
+        return carry
+
+    lax.fori_loop(0, tiles - 1, serve, 0)
+    out_ref[core, tile] = pick(tile)
+
+    def pass_copy(which, owner):
+        return remote(
+            out_ref.at[which, owner], out_ref.at[which, owner], pass_send.at[owner], pass_recv.at[owner], sibling
+        )
+
+    pass_copy(core, tile).start()
+
+    def forward(n, carry):
+        owner = lax.rem(tile + tiles - offset(n), tiles)
+        data_copy(owner, owner, owner).wait_recv()
+        pass_copy(core, owner).start()
+        return carry
+
+    lax.fori_loop(0, tiles - 1, forward, 0)
+
+    def close(n, carry):
+        pass_copy(core, n).wait_send()
+        pass_copy(1 - core, n).wait_recv()
+        return carry
+
+    lax.fori_loop(0, tiles, close, 0)
+
+    def close_sends(n, carry):
+        other = lax.rem(tile + offset(n), tiles)
+        ask_copy(other, other, other).wait_send()
+        data_copy(other, other, other).wait_send()
+        return carry
+
+    lax.fori_loop(0, tiles - 1, close_sends, 0)
+
+
+def fetch_rows(source, wanted):
+    tiles, _, share = wanted.shape
+    quarter = share // 2
+    dma = pltpu.SemaphoreType.DMA
+    return pl.pallas_call(
+        fetch_kernel,
+        out_shape=jax.ShapeDtypeStruct((2, tiles, quarter, LANES), BF),
+        in_specs=[VMEM, VMEM],
+        out_specs=VMEM,
+        scratch_shapes=[
+            pltpu.VMEM(source.shape, BF),
+            pltpu.VMEM(wanted.shape, jnp.int32),
+            pltpu.SMEM(wanted.shape, jnp.int32),
+            pltpu.VMEM((source.shape[1], LANES), F32),
+            pltpu.VMEM((quarter, LANES), F32),
+            pltpu.VMEM((tiles, quarter, LANES), BF),
+            dma((3,)), dma((tiles,)), dma((tiles,)), dma((tiles,)), dma((tiles,)), dma((tiles,)), dma((tiles,)),
+        ],
+        compiler_params=pltpu.CompilerParams(
+            collective_id=1, has_side_effects=True, vmem_limit_bytes=40 * 2**20
+        ),
+        name="fetch_rows",
+    )(source, wanted)
+
+
+def remap_kernel(chunk, entries, slots_ref, counts_ref, fetched_ref, out_ref, table_ref, rows_ref):
+    part = fetched_ref.shape[0]
+
+    def fill(block, carry):
+        at = pl.multiple_of(block * 256, 256)
+        piece = fetched_ref[pl.ds(at, 256), :].astype(F32)
+        table_ref[pl.ds(at, 256), :] = piece
+        table_ref[pl.ds(part + at, 256), :] = pltpu.roll(piece, SIDE, 1)
+        return carry
+
+    lax.fori_loop(0, part // 256, fill, 0)
+    cells = out_ref.shape[0]
 
     def step(block, carry):
         base = block * chunk
 
         def group(g, inner):
+            first = (base + g * 8) * entries
             for u in range(8):
-                at = g * 8 + u
-                left = table_ref[pl.ds(first_ref[base + at], 1), :]
-                right = table_ref[pl.ds(second_ref[base + at], 1), :]
-                rows_ref[pl.ds(at, 1), :] = jnp.where(low, left, right)
-            return inner
-
-        lax.fori_loop(0, chunk // 8, group, 0)
-        out_ref[pl.ds(pl.multiple_of(base, chunk), chunk), :] = rows_ref[...].astype(BF)
-        return carry
-
-    lax.fori_loop(0, total // chunk, step, 0)
-
-
-def pick_rows(first, second, table):
-    total = first.shape[0]
-    chunk = 128
-    return pl.pallas_call(
-        functools.partial(pick_kernel, chunk),
-        out_shape=jax.ShapeDtypeStruct((total, LANES), BF),
-        in_specs=[SMEM, SMEM, VMEM],
-        out_specs=VMEM,
-        scratch_shapes=[pltpu.VMEM((chunk, LANES), F32)],
-        compiler_params=pltpu.CompilerParams(vmem_limit_bytes=32 * 2**20),
-        name="pick_rows",
-    )(first, second, table)
-
-
-def remap_kernel(chunk, slots_ref, counts_ref, low_ref, high_ref, out_ref, table_ref, rows_ref):
-    part = low_ref.shape[0]
-
-    def fill(block, carry):
-        at = pl.multiple_of(block * 128, 128)
-        for which, ref in enumerate((low_ref, high_ref)):
-            piece = ref[pl.ds(at, 128), :].astype(F32)
-            table_ref[pl.ds(which * part + at, 128), :] = piece
-            table_ref[pl.ds((2 + which) * part + at, 128), :] = pltpu.roll(piece, SIDE, 1)
-        return carry
-
-    lax.fori_loop(0, part // 128, fill, 0)
-    entries = slots_ref.shape[0]
-    cells = out_ref.shape[0]
-
-    def step(block, carry):
-        base = block * chunk
-
-        def group(g, inner):
-            for u in range(8):
-                at = g * 8 + u
                 for k in range(entries):
-                    rows_ref[k, pl.ds(at, 1), :] = table_ref[pl.ds(slots_ref[k, base + at], 1), :]
+                    rows_ref[k, pl.ds(g * 8 + u, 1), :] = table_ref[pl.ds(slots_ref[first + (u * entries + k)], 1), :]
             return inner
 
         lax.fori_loop(0, chunk // 8, group, 0)
@@ -101,21 +213,21 @@
     lax.fori_loop(0, cells // chunk, step, 0)
 
 
-def remap_cells(slots, counts, low, high):
-    entries, cells = slots.shape
+def remap_cells(slots, counts, fetched):
+    cells, entries = counts.shape
     chunk = 128
     return pl.pallas_call(
-        functools.partial(remap_kernel, chunk),
+        functools.partial(remap_kernel, chunk, entries),
         out_shape=jax.ShapeDtypeStruct((cells, SIDE), BF),
-        in_specs=[SMEM, VMEM, VMEM, VMEM],
+        in_specs=[SMEM, VMEM, VMEM],
         out_specs=VMEM,
         scratch_shapes=[
-            pltpu.VMEM((4 * low.shape[0], LANES), F32),
+            pltpu.VMEM((2 * fetched.shape[0], LANES), F32),
             pltpu.VMEM((entries, chunk, LANES), F32),
         ],
         compiler_params=pltpu.CompilerParams(vmem_limit_bytes=40 * 2**20),
         name="remap_cells",
-    )(slots, counts, low, high)
+    )(slots, counts, fetched)
 
 
 def seam_choice(seam, position, core, height):
@@ -335,20 +447,7 @@
     cells_half = cell_slots.shape[2] // 2
 
     requests = lax.dynamic_slice_in_dim(request_rows[0], core * share, share, 1)
-    wanted = lax.all_to_all(requests, "tile", split_axis=0, concat_axis=0, tiled=True)
-    sibling = swap_core(source)
-    rows = jnp.where(
-        core == 0, jnp.concatenate([source, sibling]), jnp.concatenate([sibling, source])
-    ).T.astype(F32)
-    table = jnp.concatenate([rows, rows], axis=1)
-    wanted = wanted.reshape(tiles, 2, quarter)
-    picked = pick_rows(wanted[:, 0].reshape(-1), wanted[:, 1].reshape(-1), table)
-    arrived = lax.all_to_all(
-        picked.reshape(tiles, quarter, LANES), "tile", split_axis=0, concat_axis=0, tiled=True
-    ).reshape(tiles * quarter, LANES)
-    across = swap_core(arrived)
-    low = jnp.where(core == 0, arrived, across)
-    high = jnp.where(core == 0, across, arrived)
+    fetched = fetch_rows(source, requests[:, None, :]).reshape(2 * tiles * quarter, LANES)
 
     slots = lax.dynamic_slice_in_dim(cell_slots[0], core * cells_half, cells_half, 1)
     counts = lax.dynamic_slice_in_dim(cell_counts[0], core * cells_half, cells_half, 1)
@@ -356,7 +455,7 @@
     served, inside = place // share, place % share
     part = tiles * quarter
     table_rows = (inside // quarter) * (2 * part) + served * part + owner * quarter + inside % quarter
-    remapped = remap_cells(table_rows, counts.astype(F32).T, low, high)
+    remapped = remap_cells(table_rows.T.reshape(-1), counts.astype(F32).T, fetched)
 
     choice = seam_choice(seam, position, core, cells_half // SIDE)
 

time: 108 us -> 94.6 us (0.88)
  Pallas kernels: 52.1 us -> 77.5 us
  waiting for transfers between devices: 18.1 us -> 0 us
  starting transfers between devices: 11.4 us -> 0 us
  other arithmetic: 6.28 us -> 1.25 us
  local copies, waits for them, and re-layouts: 8.42 us -> 4.67 us
    pallas_call x2, Pallas kernels: 31 us -> 56.6 us  [the longest x1 41 us: fetch_rows(): pl.pallas_call(fetch_kernel, out_shape=jax.ShapeDtypeStruct((2, tiles, qu...]
    all_to_all x2 -> x0, waiting for transfers between devices: 15.9 us -> none  [the longest x1 11.2 us: shards(): lax.all_to_all(picked.reshape(tiles, quarter, LANES), 'tile', split_axis=...]
    all_to_all x2 -> x0, starting transfers between devices: 11 us -> none  [the longest x1 7.25 us: shards(): lax.all_to_all(requests, 'tile', split_axis=0, concat_axis=0, tiled=True)]
    convert_element_type x1 -> x0, other arithmetic: 4.52 us -> none  [shards(): rows = jnp.where(core == 0, jnp.concatenate([source, sibling]), jnp.conca...]
    unnamed x19 -> x18, local copies, waits for them, and re-layouts: 3.41 us -> 1.11 us
    ppermute x2 -> x0, waiting for transfers between devices: 2.21 us -> none  [swap_core(): return lax.ppermute(x, 'ch', [(0, 1), (1, 0)])]
    ppermute x1 -> x0, local copies, waits for them, and re-layouts: 1.75 us -> none  [swap_core(): return lax.ppermute(x, 'ch', [(0, 1), (1, 0)])]
  transfers between devices with their start and end apart: 4 -> 0, of which waited for: 3 -> 0; matrix products, arithmetic and copies ran while one was open for 5% -> 0% of each run, Pallas kernels for 0% -> 0%
where the time goes in v3:
time: 94.6 us; the launch traced here: 94.3 us
  Pallas kernels  77.5 us (82%)
  between operations  10.9 us (12%)
  local copies, waits for them, and re-layouts  4.67 us (5%)
  other arithmetic  1.25 us (1%)
    pallas_call x1, Pallas kernels, fetch_rows(): pl.pallas_call(fetch_kernel, out_shape=jax.ShapeDtypeStruct((2, tiles, qu...  41 us
    pallas_call x1, Pallas kernels, conv_block(): pl.pallas_call(kernel, out_shape=jax.ShapeDtypeStruct((chans // 2, 2 * ce...  20.9 us
    pallas_call x1, Pallas kernels, remap_cells(): pl.pallas_call(functools.partial(remap_kernel, chunk, entries), out_shape...  15.6 us
    slice x4, local copies, waits for them, and re-layouts, seam_choice(): lax.dynamic_index_in_dim(seam, (position + by) % tiles, 0, keepdims=False)  2.05 us

profile of v3, /device:TPU:0, one launch (start us, length us, event | category | flops | bytes accessed | tf_op | source)
XLA Modules:
  0.0 94.3 jit_solution(4398218403457836030)
XLA Ops:
  0.0 0.0 copy-start
  0.0 1.0 %fusion.5 = s32[2048,4]{0,1:T(4,128)S(1)} fusion(s32[1,4,4096]{2,1,0:T(4,128)} %param.11, s32[]{:T(128)S(6)} %select_n.211), kind=kLoop, calls=%fused_computation.22 | loop fusion | flops 516096 | bytes 65540 | tf_op jit(solution)/shard_map/transpose | solution.py:458
  1.0 0.4 copy.16
  1.3 0.0 copy-start.6
  1.4 0.0 copy-start.1
  1.4 0.6 reshape.27.slots_ref
  2.0 0.0 copy-done
  2.0 0.4 copy.20
  2.4 0.1 convert_bitcast_fusion.counts_ref
  2.5 0.0 copy-done.6
  2.5 0.0 copy-done.1
  2.6 41.0 %fetch_rows.1 = bf16[2,8,512,128]{3,2,1,0:T(8,128)(2,1)S(1)} custom-call(bf16[32,8192]{1,0:T(8,128)(2,1)S(1)} %copy-done.1, s32[8,1,1024]{2,1,0:T(1,128)S(1)} %broadcast_in_dim.29.wanted_ref), custom_call_target="tpu_custom_call" | custom-call | tf_op jit(solution)/shard_map/fetch_rows/pallas_call | solution.py:158
  43.6 0.0 copy-start.5
  43.6 0.0 copy-start.4
  43.6 0.0 copy-start.7
  43.6 0.0 copy-start.3
  43.6 0.0 copy-start.2
  43.6 15.6 %remap_cells.1.refs_0_ = bf16[2048,64]{1,0:T(8,128)(2,1)S(1)} custom-call(s32[8192]{0:T(1024)S(1)} %reshape.27.slots_ref, f32[2048,4]{1,0:T(8,128)S(1)} %convert_bitcast_fusion.counts_ref, bf16[8192,128]{1,0:T(8,128)(2,1)S(1)} %bitcast.33), custom_call_target="tpu_custom_call" | custom-call | tf_op jit(solution)/shard_map/remap_cells/pallas_call | solution.py:219
  59.3 0.0 copy-done.5
  59.3 0.1 constant_dynamic-slice_fusion.3
  59.4 0.5 slice.19
  62.5 0.5 slice.18
  65.7 0.5 slice.17
  68.9 0.5 slice.16
  72.0 0.1 pad_add_fusion
  72.1 0.1 fusion.refs_1_
  72.2 0.0 copy-done.4
  72.2 0.1 copy.18
  72.4 0.0 copy-done.7
  72.4 0.0 copy-done.3
  72.4 0.2 copy.19
  72.6 0.0 copy-done.2
  72.6 20.9 %conv_block.1 = bf16[32,4096]{1,0:T(8,128)(2,1)S(1)} custom-call(bf16[2048,64]{1,0:T(8,128)(2,1)S(1)} %remap_cells.1.refs_0_, bf16[256,192]{1,0:T(8,128)(2,1)S(1)} %fusion.refs_1_, bf16[9,64,64]{2,1,0:T(8,128)(2,1)S(1)} %bitcast.36, f32[8,64]{1,0:T(8,128)S(1)} %broadcast_in_dim.31.refs_3_, bf16[9,128,64]{2,1,0:T(8,128)(2,1)S(1)} %bitcast.34, ...), custom_call_target="tpu_custom_call" | custom-call | tf_op jit(solution)/shard_map/conv_block/pallas_call | solution.py:415
  93.6 0.7 copy.22
  (6 shorter events, 0.1 us)
Async XLA Ops:
  0.0 2.0 %copy-start = (s32[1,4,4096]{2,1,0:T(4,128)S(1)}, s32[1,4,4096]{2,1,0:T(4,128)}, u32[]{:S(2)}) copy-start(s32[1,4,4096]{2,1,0:T(4,128)} %param.12) | copy-start | bytes 196612
  1.3 1.1 %copy-start.6 = (s32[1,8,2048]{2,1,0:T(8,128)S(1)}, s32[1,8,2048]{2,1,0:T(8,128)}, u32[]{:S(2)}) copy-start(s32[1,8,2048]{2,1,0:T(8,128)} %param.10) | copy-start | bytes 196612
  1.4 1.2 %copy-start.1 = (bf16[32,8192]{1,0:T(8,128)(2,1)S(1)}, bf16[32,8192]{1,0:T(8,128)(2,1)}, u32[]{:S(2)}) copy-start(bf16[32,8192]{1,0:T(8,128)(2,1)} %source_ref.1) | copy-start | bytes 1572868
  43.6 15.7 %copy-start.5 = (s32[8,4]{0,1:T(4,128)S(1)}, s32[8,4]{0,1:T(4,128)}, u32[]{:S(2)}) copy-start(s32[8,4]{0,1:T(4,128)} %param.13) | copy-start | bytes 388
  43.6 28.6 %copy-start.4 = (bf16[3,3,64,64]{3,2,1,0:T(8,128)(2,1)S(1)}, bf16[3,3,64,64]{3,2,1,0:T(8,128)(2,1)}, u32[]{:S(2)}) copy-start(bf16[3,3,64,64]{3,2,1,0:T(8,128)(2,1)} %param.14) | copy-start | bytes 221188
  43.6 28.8 %copy-start.7 = (f32[64]{0:T(128)S(1)}, f32[64]{0:T(128)}, u32[]{:S(2)}) copy-start(f32[64]{0:T(128)} %param.15) | copy-start | bytes 772
  43.6 28.8 %copy-start.3 = (bf16[3,3,64,128]{3,2,1,0:T(8,128)(2,1)S(1)}, bf16[3,3,64,128]{3,2,1,0:T(8,128)(2,1)}, u32[]{:S(2)}) copy-start(bf16[3,3,64,128]{3,2,1,0:T(8,128)(2,1)} %param.16) | copy-start | bytes 442372
  43.6 29.0 %copy-start.2 = (f32[64]{0:T(128)S(1)}, f32[64]{0:T(128)}, u32[]{:S(2)}) copy-start(f32[64]{0:T(128)} %param.17) | copy-start | bytes 772

commit v4 on v3

--- a/solution.py
+++ b/solution.py
@@ -27,14 +27,21 @@
     sibling = (grp, tile, 1 - core)
     quarter = rows_ref.shape[0]
 
-    def offset(n):
-        return 1 + lax.rem(n + tiles // 2 - 1, tiles - 1)
+    middle = tiles // 2
+    side_start = tile // middle * middle
+    across = middle - side_start
+    place = lax.rem(tile, middle)
+
+    def partner(n, sign=1):
+        far = 1 - n // middle
+        base = far * across + (1 - far) * side_start
+        return base + lax.rem(place + middle + sign * (lax.rem(n, middle) + 1 - far), middle)
 
     barrier = pltpu.get_barrier_semaphore()
     pl.semaphore_signal(barrier, inc=1, device_id=sibling, device_id_type=mesh_id)
 
     def greet(n, carry):
-        other = lax.rem(tile + offset(n), tiles)
+        other = partner(n)
         pl.semaphore_signal(barrier, inc=1, device_id=(grp, other, core), device_id_type=mesh_id)
         return carry
 
@@ -56,7 +63,7 @@
         )
 
     def ask(n, carry):
-        owner = lax.rem(tile + offset(n), tiles)
+        owner = partner(n)
         ask_copy(owner, tile, tile).start()
         return carry
 
@@ -64,7 +71,7 @@
     asked[tile] = wanted_ref[tile]
 
     def answered(n, carry):
-        asker = lax.rem(tile + offset(n), tiles)
+        asker = partner(n)
         ask_copy(asker, asker, asker).wait_recv()
         return carry
 
@@ -112,7 +119,7 @@
         )
 
     def serve(n, carry):
-        asker = lax.rem(tile + offset(n), tiles)
+        asker = partner(n)
         send_ref[asker] = pick(asker)
         data_copy(asker, tile, tile).start()
         return carry
@@ -128,7 +135,7 @@
     pass_copy(core, tile).start()
 
     def forward(n, carry):
-        owner = lax.rem(tile + tiles - offset(n), tiles)
+        owner = partner(n, -1)
         data_copy(owner, owner, owner).wait_recv()
         pass_copy(core, owner).start()
         return carry
@@ -143,7 +150,7 @@
     lax.fori_loop(0, tiles, close, 0)
 
     def close_sends(n, carry):
-        other = lax.rem(tile + offset(n), tiles)
+        other = partner(n)
         ask_copy(other, other, other).wait_send()
         data_copy(other, other, other).wait_send()
         return carry
@@ -176,7 +183,7 @@
     )(source, wanted)
 
 
-def remap_kernel(chunk, entries, slots_ref, counts_ref, fetched_ref, out_ref, table_ref, rows_ref):
+def remap_into(chunk, entries, slots_ref, counts_ref, fetched_ref, field, body, table_ref, rows_ref):
     part = fetched_ref.shape[0]
 
     def fill(block, carry):
@@ -187,7 +194,7 @@
         return carry
 
     lax.fori_loop(0, part // 256, fill, 0)
-    cells = out_ref.shape[0]
+    cells = counts_ref.shape[0]
 
     def step(block, carry):
         base = block * chunk
@@ -200,55 +207,39 @@
             return inner
 
         lax.fori_loop(0, chunk // 8, group, 0)
-        here = pl.ds(pl.multiple_of(base, chunk), chunk)
-        weights = counts_ref[here, :]
+        weights = counts_ref[pl.ds(pl.multiple_of(base, chunk), chunk), :]
         count = weights[:, 0:1]
         summed = weights[:, 0:1] * rows_ref[0]
         for k in range(1, entries):
             count = count + weights[:, k : k + 1]
             summed = summed + weights[:, k : k + 1] * rows_ref[k]
-        out_ref[here, :] = (summed / count)[:, :SIDE].astype(BF)
+        cell = (summed / count)[:, :SIDE].astype(BF).astype(F32)
+        field[pl.ds(pl.multiple_of(body + base, 8), chunk), :] = cell
         return carry
 
     lax.fori_loop(0, cells // chunk, step, 0)
 
 
-def remap_cells(slots, counts, fetched):
-    cells, entries = counts.shape
-    chunk = 128
-    return pl.pallas_call(
-        functools.partial(remap_kernel, chunk, entries),
-        out_shape=jax.ShapeDtypeStruct((cells, SIDE), BF),
-        in_specs=[SMEM, VMEM, VMEM],
-        out_specs=VMEM,
-        scratch_shapes=[
-            pltpu.VMEM((2 * fetched.shape[0], LANES), F32),
-            pltpu.VMEM((entries, chunk, LANES), F32),
-        ],
-        compiler_params=pltpu.CompilerParams(vmem_limit_bytes=40 * 2**20),
-        name="remap_cells",
-    )(slots, counts, fetched)
-
-
-def seam_choice(seam, position, core, height):
-    tiles = seam.shape[0]
-    place = jnp.arange(SIDE, dtype=jnp.int32)
-    rows = []
-    for side, by in enumerate(MOVES):
-        code = lax.dynamic_index_in_dim(seam, (position + by) % tiles, 0, keepdims=False)[side]
+def choose_edges(codes, core, height, width, choice):
+    i = lax.broadcasted_iota(jnp.int32, (SIDE, width), 0)
+    lane = lax.broadcasted_iota(jnp.int32, (SIDE, width), 1)
+    for d, code in enumerate(codes):
+        flip = code // 4
         edge = code % 4
-        cell = jnp.where(code >= 4, SIDE - 1 - place, place)
+        is_column = edge % 2
+        second = edge // 2
+        cell = i + flip * (SIDE - 1 - 2 * i)
         near = cell - core * height
-        column = jnp.where((near >= 0) & (near < height), 2 * SIDE + jnp.where(edge == 1, height, 0) + near, -1)
-        row = jnp.where(core == edge // 2, core * SIDE + cell, -1)
-        rows.append(jnp.where(edge % 2 == 0, row, column))
-    wanted = jnp.concatenate(rows)
-    width = 2 * SIDE + 2 * height
-    return (wanted[:, None] == jnp.arange(width, dtype=jnp.int32)[None, :]).astype(BF)
+        in_column = (lane == near + (2 * SIDE + (1 - second) * height)) & (near >= 0) & (near < height)
+        in_row = lane == cell + core * SIDE
+        row_here = (1 - is_column) * (second * core + (1 - second) * (1 - core))
+        hit = in_column.astype(jnp.int32) * is_column + in_row.astype(jnp.int32) * row_here
+        choice[d * SIDE : (d + 1) * SIDE, :] = hit.astype(F32).astype(BF)
 
 
 def block_kernel(
-    half_ref, choice_ref, first_ref, first_bias_ref, second_ref, second_bias_ref, out_ref,
+    slots_ref, counts_ref, fetched_ref, seam_ref, first_ref, first_bias_ref, second_ref, second_bias_ref, out_ref,
+    table_ref, rows_ref, choice_ref,
     field, hidden, west_buf, east_buf, left_shift, right_shift, mid_buf, pack_one, pack_two,
     send_one, send_two, recv_one, recv_two, halo_one, halo_two, other_first, other_bias,
     first_full, turned, send_sems, recv_sems, side_sems,
@@ -257,7 +248,7 @@
     tiles = lax.axis_size("tile")
     sibling = (grp, tile, 1 - core)
     upper = core == 0
-    cells = half_ref.shape[0]
+    cells = counts_ref.shape[0]
     height = cells // SIDE
     rows = cells + 2 * SIDE
     start = 8
@@ -271,7 +262,10 @@
         for c in range(2):
             pl.semaphore_signal(barrier, inc=1, device_id=(grp, other, c), device_id_type=pl.DeviceIdType.MESH)
 
-    field[pl.ds(body, cells), :] = half_ref[...].astype(F32)
+    codes = [seam_ref[targets[d], d] for d in range(4)]
+    choose_edges(codes, core, height, choice_ref.shape[1], choice_ref)
+    entries = counts_ref.shape[1]
+    remap_into(128, entries, slots_ref, counts_ref, fetched_ref, field, body, table_ref, rows_ref)
     pl.semaphore_wait(barrier, 9)
 
     def remote(src, dst, send_sem, recv_sem, device):
@@ -306,6 +300,11 @@
             copy.start()
         return copies
 
+    def prepare(grid, left, right, mid, width):
+        left[SIDE : SIDE + cells, :] = grid[body - 1 : body - 1 + cells, :]
+        right[SIDE : SIDE + cells, :] = grid[body + 1 : body + 1 + cells, :]
+        mid[1, SIDE : SIDE + cells, 0:width] = grid[body : body + cells, :].astype(BF)
+
     def finish(rnd, copies, grid, send, recv, halo, left, right, mid, width):
         lanes = slice(0, width)
         for d in range(4):
@@ -333,12 +332,13 @@
 
         west_cells = column(west_buf, west, 0)
         east_cells = column(east_buf, east, SIDE - 1)
-        left[...] = grid[start - 1 : start - 1 + rows, :]
+        for at in (0, SIDE + cells):
+            left[at : at + SIDE, :] = grid[start + at - 1 : start + at - 1 + SIDE, :]
+            right[at : at + SIDE, :] = grid[start + at + 1 : start + at + 1 + SIDE, :]
+            mid[1, at : at + SIDE, lanes] = grid[start + at : start + at + SIDE, :].astype(BF)
         left[pl.ds(0, height + 2, stride=SIDE), :] = west_cells
-        right[...] = grid[start + 1 : start + 1 + rows, :]
         right[pl.ds(SIDE - 1, height + 2, stride=SIDE), :] = east_cells
         mid[0, :, lanes] = left[...].astype(BF)
-        mid[1, :, lanes] = grid[start : start + rows, :].astype(BF)
         mid[2, :, lanes] = right[...].astype(BF)
         for copy in copies:
             copy.wait_send()
@@ -356,9 +356,10 @@
 
     weight_copy = remote(first_ref, other_first, side_sems.at[0], side_sems.at[1], sibling)
     bias_copy = remote(first_bias_ref, other_bias, side_sems.at[2], side_sems.at[3], sibling)
-    copies = begin(0, field, pack_one, send_one, recv_one, halo_one)
     weight_copy.start()
     bias_copy.start()
+    copies = begin(0, field, pack_one, send_one, recv_one, halo_one)
+    prepare(field, left_shift[0], right_shift[0], mid_buf, SIDE)
     weight_copy.wait()
     bias_copy.wait()
     mine, other = first_ref[...], other_first[...]
@@ -377,6 +378,7 @@
 
     lax.fori_loop(0, cells // block, first, 0)
     copies = begin(1, hidden, pack_two, send_two, recv_two, halo_two)
+    prepare(hidden, left_shift[1], right_shift[1], mid_buf, 2 * SIDE)
     finish(1, copies, hidden, send_two, recv_two, halo_two, left_shift[1], right_shift[1], mid_buf, 2 * SIDE)
 
     def second(step, carry):
@@ -400,24 +402,27 @@
     away.wait()
 
 
-def conv_block(half, choice, first, first_bias, second, second_bias):
-    cells, chans = half.shape
+def conv_block(slots, counts, fetched, seam, first, first_bias, second, second_bias):
+    cells, entries = counts.shape
+    chans = first.shape[1]
     hid = 2 * chans
     rows = cells + 2 * SIDE
-    pack = choice.shape[1]
+    pack = 2 * SIDE + 2 * (cells // SIDE)
     shape = pltpu.VMEM
 
     def kernel(*refs):
-        ins, rest = refs[:7], list(refs[7:])
+        ins, rest = refs[:12], list(refs[12:])
         l1, l2, r1, r2 = rest[4:8]
         block_kernel(*ins, *rest[:4], (l1, l2), (r1, r2), *rest[8:])
 
     return pl.pallas_call(
         kernel,
         out_shape=jax.ShapeDtypeStruct((chans // 2, 2 * cells), BF),
-        in_specs=[VMEM] * 6,
+        in_specs=[SMEM, VMEM, VMEM, SMEM, VMEM, VMEM, VMEM, VMEM],
         out_specs=VMEM,
         scratch_shapes=[
+            shape((2 * fetched.shape[0], LANES), F32), shape((entries, 128, LANES), F32),
+            shape((4 * SIDE, pack), BF),
             shape((rows + 16, chans), F32), shape((rows + 16, hid), F32),
             shape((SIDE + 16, hid), F32), shape((SIDE + 16, hid), F32),
             shape((rows, chans), F32), shape((rows, hid), F32),
@@ -435,11 +440,10 @@
             collective_id=0, has_side_effects=True, vmem_limit_bytes=48 * 2**20
         ),
         name="conv_block",
-    )(half, choice, first, first_bias, second, second_bias)
+    )(slots, counts, fetched, seam, first, first_bias, second, second_bias)
 
 
 def shards(source, request_rows, cell_slots, cell_counts, seam, conv_first, bias_first, conv_second, bias_second):
-    position = lax.axis_index("tile")
     core = lax.axis_index("ch")
     tiles, slots_each = request_rows.shape[1], request_rows.shape[2]
     share = slots_each // 2
@@ -455,16 +459,13 @@
     served, inside = place // share, place % share
     part = tiles * quarter
     table_rows = (inside // quarter) * (2 * part) + served * part + owner * quarter + inside % quarter
-    remapped = remap_cells(table_rows.T.reshape(-1), counts.astype(F32).T, fetched)
-
-    choice = seam_choice(seam, position, core, cells_half // SIDE)
-
     def arrange(weights):
         return jnp.transpose(weights, (0, 1, 3, 2)).reshape(9, weights.shape[3], weights.shape[2])
 
     bias_rows = jnp.broadcast_to(bias_first[None], (8, bias_first.shape[0]))
     return conv_block(
-        remapped, choice, arrange(conv_first), bias_rows, arrange(conv_second), bias_second[None]
+        table_rows.T.reshape(-1), counts.astype(F32).T, fetched, seam,
+        arrange(conv_first), bias_rows, arrange(conv_second), bias_second[None],
     )[None]
 
 

time: 94.6 us -> 84.4 us (0.89)
  between operations: 10.9 us -> 0.07 us
  local copies, waits for them, and re-layouts: 4.67 us -> 6.51 us
  Pallas kernels: 77.5 us -> 76.5 us
    pallas_call x1 -> x0, Pallas kernels: 15.6 us -> none  [remap_cells(): pl.pallas_call(functools.partial(remap_kernel, chunk, entries), out_shape...]
    pallas_call x1, Pallas kernels: 20.9 us -> 34 us  [conv_block(): pl.pallas_call(kernel, out_shape=jax.ShapeDtypeStruct((chans // 2, 2 * ce...]
    slice x4 -> x0, local copies, waits for them, and re-layouts: 2.05 us -> none  [seam_choice(): lax.dynamic_index_in_dim(seam, (position + by) % tiles, 0, keepdims=False)]
    transpose x2, local copies, waits for them, and re-layouts: 0.38 us -> 2.18 us  [arrange(): jnp.transpose(weights, (0, 1, 3, 2))]
    pallas_call x1, Pallas kernels: 41 us -> 42.5 us  [fetch_rows(): pl.pallas_call(fetch_kernel, out_shape=jax.ShapeDtypeStruct((2, tiles, qu...]
where the time goes in v4:
time: 84.4 us; the launch traced here: 84.1 us
  Pallas kernels  76.5 us (91%)
  local copies, waits for them, and re-layouts  6.51 us (8%)
  other arithmetic  1.02 us (1%)
    pallas_call x1, Pallas kernels, fetch_rows(): pl.pallas_call(fetch_kernel, out_shape=jax.ShapeDtypeStruct((2, tiles, qu...  42.5 us
    pallas_call x1, Pallas kernels, conv_block(): pl.pallas_call(kernel, out_shape=jax.ShapeDtypeStruct((chans // 2, 2 * ce...  34 us
    transpose x2, local copies, waits for them, and re-layouts, arrange(): jnp.transpose(weights, (0, 1, 3, 2))  2.18 us
    unnamed x9, local copies, waits for them, and re-layouts  1.88 us

profile of v4, /device:TPU:0, one launch (start us, length us, event | category | flops | bytes accessed | tf_op | source)
XLA Modules:
  0.0 84.1 jit_solution(10404308861960426184)
XLA Ops:
  0.0 0.0 copy-start
  0.0 0.8 copy.22.refs_3_
  0.8 0.7 broadcast_in_dim.16.refs_5_
  1.4 0.0 copy-done
  1.5 0.9 %fusion.4 = s32[2048,4]{0,1:T(4,128)S(1)} fusion(s32[1,4,4096]{2,1,0:T(4,128)} %param.11, s32[]{:T(128)S(6)} %select_n.33), kind=kLoop, calls=%fused_computation.20 | loop fusion | flops 516096 | bytes 65540 | tf_op jit(solution)/shard_map/transpose | solution.py:467
  2.4 0.8 constant_dynamic-slice_fusion
  3.2 1.0 %copy.20 = bf16[3,3,64,64]{3,2,1,0:T(8,128)(2,1)S(1)} copy(bf16[3,3,64,64]{2,3,1,0:T(8,128)(2,1)} %bitcast.35) | data formatting | bytes 147456 | tf_op jit(solution)/shard_map/transpose | solution.py:463
  4.2 1.1 %copy.21 = bf16[3,3,128,64]{3,2,1,0:T(8,128)(2,1)S(1)} copy(bf16[3,3,128,64]{2,3,1,0:T(8,128)(2,1)} %bitcast.34) | data formatting | bytes 294912 | tf_op jit(solution)/shard_map/transpose | solution.py:463
  5.4 0.4 copy.23
  5.8 0.0 copy-start.1
  5.8 0.1 convert_bitcast_fusion.refs_1_
  5.8 0.4 copy.18
  6.2 0.0 copy-start.2
  6.2 0.6 reshape.18.refs_0_
  6.9 0.0 copy-done.1
  6.9 42.5 %fetch_rows.1 = bf16[2,8,512,128]{3,2,1,0:T(8,128)(2,1)S(1)} custom-call(bf16[32,8192]{1,0:T(8,128)(2,1)S(1)} %copy-done.1, s32[8,1,1024]{2,1,0:T(1,128)S(1)} %broadcast_in_dim.15.wanted_ref), custom_call_target="tpu_custom_call" | custom-call | tf_op jit(solution)/shard_map/fetch_rows/pallas_call | solution.py:165
  49.3 0.0 copy-done.2
  49.3 34.0 %conv_block.1 = bf16[32,4096]{1,0:T(8,128)(2,1)S(1)} custom-call(s32[8192]{0:T(1024)S(1)} %reshape.18.refs_0_, f32[2048,4]{1,0:T(8,128)S(1)} %convert_bitcast_fusion.refs_1_, bf16[8192,128]{1,0:T(8,128)(2,1)S(1)} %bitcast.29, s32[8,4]{1,0:T(8,128)S(1)} %copy.22.refs_3_, bf16[9,64,64]{2,1,0:T(8,128)(2,1)S(1)} %bitcast.32, ...), custom_call_target="tpu_custom_call" | custom-call | tf_op jit(solution)/shard_map/conv_block/pallas_call | solution.py:418
  83.4 0.7 copy.25
  (2 shorter events, 0.0 us)
Async XLA Ops:
  0.0 1.4 %copy-start = (s32[1,8,2048]{2,1,0:T(8,128)S(1)}, s32[1,8,2048]{2,1,0:T(8,128)}, u32[]{:S(2)}) copy-start(s32[1,8,2048]{2,1,0:T(8,128)} %param.10) | copy-start | bytes 196612
  5.8 1.1 %copy-start.1 = (bf16[32,8192]{1,0:T(8,128)(2,1)S(1)}, bf16[32,8192]{1,0:T(8,128)(2,1)}, u32[]{:S(2)}) copy-start(bf16[32,8192]{1,0:T(8,128)(2,1)} %source_ref.1) | copy-start | bytes 1572868
  6.2 43.1 %copy-start.2 = (f32[64]{0:T(128)S(1)}, f32[64]{0:T(128)}, u32[]{:S(2)}) copy-start(f32[64]{0:T(128)} %param.17) | copy-start | bytes 772

commit v5 on v4

--- a/solution.py
+++ b/solution.py
@@ -183,7 +183,7 @@
     )(source, wanted)
 
 
-def remap_into(chunk, entries, slots_ref, counts_ref, fetched_ref, field, body, table_ref, rows_ref):
+def remap_into(chunk, entries, slots_copy, slots_here, counts_ref, fetched_ref, field, body, table_ref, rows_ref):
     part = fetched_ref.shape[0]
 
     def fill(block, carry):
@@ -194,16 +194,17 @@
         return carry
 
     lax.fori_loop(0, part // 256, fill, 0)
+    slots_copy.wait()
     cells = counts_ref.shape[0]
 
     def step(block, carry):
         base = block * chunk
 
         def group(g, inner):
-            first = (base + g * 8) * entries
+            first = base + g * 8
             for u in range(8):
                 for k in range(entries):
-                    rows_ref[k, pl.ds(g * 8 + u, 1), :] = table_ref[pl.ds(slots_ref[first + (u * entries + k)], 1), :]
+                    rows_ref[k, pl.ds(g * 8 + u, 1), :] = table_ref[pl.ds(slots_here[k, 0, first + u], 1), :]
             return inner
 
         lax.fori_loop(0, chunk // 8, group, 0)
@@ -238,8 +239,9 @@
 
 
 def block_kernel(
+    cap,
     slots_ref, counts_ref, fetched_ref, seam_ref, first_ref, first_bias_ref, second_ref, second_bias_ref, out_ref,
-    table_ref, rows_ref, choice_ref,
+    table_ref, rows_ref, choice_ref, slots_moved, slots_here, second_full,
     field, hidden, west_buf, east_buf, left_shift, right_shift, mid_buf, pack_one, pack_two,
     send_one, send_two, recv_one, recv_two, halo_one, halo_two, other_first, other_bias,
     first_full, turned, send_sems, recv_sems, side_sems,
@@ -258,6 +260,16 @@
 
     barrier = pltpu.get_barrier_semaphore()
     pl.semaphore_signal(barrier, inc=1, device_id=sibling, device_id_type=pl.DeviceIdType.MESH)
+    slot = slots_ref[:, pl.ds(pl.multiple_of(core * cells, cells), cells)]
+    part = fetched_ref.shape[0]
+    owner, inside = slot // cap, slot % cap
+    served, inside = inside // (cap // 2), inside % (cap // 2)
+    group, inside = inside // (cap // 4), inside % (cap // 4)
+    at_row = group * part + served * (part // 2) + owner * (cap // 4) + inside
+    for k in range(slots_ref.shape[0]):
+        slots_moved[k] = at_row[k : k + 1]
+    slots_copy = pltpu.make_async_copy(slots_moved, slots_here, side_sems.at[6])
+    slots_copy.start()
     for other in targets:
         for c in range(2):
             pl.semaphore_signal(barrier, inc=1, device_id=(grp, other, c), device_id_type=pl.DeviceIdType.MESH)
@@ -265,7 +277,9 @@
     codes = [seam_ref[targets[d], d] for d in range(4)]
     choose_edges(codes, core, height, choice_ref.shape[1], choice_ref)
     entries = counts_ref.shape[1]
-    remap_into(128, entries, slots_ref, counts_ref, fetched_ref, field, body, table_ref, rows_ref)
+    for k in range(9):
+        second_full[k] = second_ref[k].astype(F32).T.astype(BF)
+    remap_into(128, entries, slots_copy, slots_here, counts_ref, fetched_ref, field, body, table_ref, rows_ref)
     pl.semaphore_wait(barrier, 9)
 
     def remote(src, dst, send_sem, recv_sem, device):
@@ -363,9 +377,11 @@
     weight_copy.wait()
     bias_copy.wait()
     mine, other = first_ref[...], other_first[...]
-    first_full[:, :, 0:SIDE] = jnp.where(upper, mine, other)
-    first_full[:, :, SIDE:] = jnp.where(upper, other, mine)
-    mine, other = first_bias_ref[0:1, :], other_bias[0:1, :]
+    for k in range(9):
+        one, two = mine[k].astype(F32), other[k].astype(F32)
+        both = jnp.concatenate([jnp.where(upper, one, two), jnp.where(upper, two, one)])
+        first_full[k] = both.T.astype(BF)
+    mine, other = first_bias_ref[...], other_bias[...]
     bias = jnp.concatenate([jnp.where(upper, mine, other), jnp.where(upper, other, mine)], axis=1)
     finish(0, copies, field, send_one, recv_one, halo_one, left_shift[0], right_shift[0], mid_buf, SIDE)
 
@@ -383,7 +399,7 @@
 
     def second(step, carry):
         at = pl.multiple_of(step * block, block)
-        v = convolve(mid_buf, second_ref, at, 2 * SIDE) + second_bias_ref[...]
+        v = convolve(mid_buf, second_full, at, 2 * SIDE) + second_bias_ref[...]
         v = v + field[pl.ds(pl.multiple_of(body + at, 8), block), :]
         turned[:, pl.ds(at, block)] = v.T.astype(BF)
         return carry
@@ -402,27 +418,28 @@
     away.wait()
 
 
-def conv_block(slots, counts, fetched, seam, first, first_bias, second, second_bias):
+def conv_block(cap, slots, counts, fetched, seam, first, first_bias, second, second_bias):
     cells, entries = counts.shape
-    chans = first.shape[1]
+    chans = first.shape[2]
     hid = 2 * chans
     rows = cells + 2 * SIDE
     pack = 2 * SIDE + 2 * (cells // SIDE)
     shape = pltpu.VMEM
 
     def kernel(*refs):
-        ins, rest = refs[:12], list(refs[12:])
+        ins, rest = refs[:15], list(refs[15:])
         l1, l2, r1, r2 = rest[4:8]
-        block_kernel(*ins, *rest[:4], (l1, l2), (r1, r2), *rest[8:])
+        block_kernel(cap, *ins, *rest[:4], (l1, l2), (r1, r2), *rest[8:])
 
     return pl.pallas_call(
         kernel,
         out_shape=jax.ShapeDtypeStruct((chans // 2, 2 * cells), BF),
-        in_specs=[SMEM, VMEM, VMEM, SMEM, VMEM, VMEM, VMEM, VMEM],
+        in_specs=[VMEM, VMEM, VMEM, SMEM, VMEM, VMEM, VMEM, VMEM],
         out_specs=VMEM,
         scratch_shapes=[
             shape((2 * fetched.shape[0], LANES), F32), shape((entries, 128, LANES), F32),
-            shape((4 * SIDE, pack), BF),
+            shape((4 * SIDE, pack), BF), shape((entries, 1, cells), jnp.int32),
+            pltpu.SMEM((entries, 1, cells), jnp.int32), shape((9, hid, chans), BF),
             shape((rows + 16, chans), F32), shape((rows + 16, hid), F32),
             shape((SIDE + 16, hid), F32), shape((SIDE + 16, hid), F32),
             shape((rows, chans), F32), shape((rows, hid), F32),
@@ -434,7 +451,7 @@
             shape((SIDE, chans), BF), shape((SIDE, hid), BF),
             shape(first.shape, BF), shape(first_bias.shape, F32),
             shape((9, chans, hid), BF), shape((chans, cells), BF),
-            pltpu.SemaphoreType.DMA((2, 9)), pltpu.SemaphoreType.DMA((2, 9)), pltpu.SemaphoreType.DMA((6,)),
+            pltpu.SemaphoreType.DMA((2, 9)), pltpu.SemaphoreType.DMA((2, 9)), pltpu.SemaphoreType.DMA((7,)),
         ],
         compiler_params=pltpu.CompilerParams(
             collective_id=0, has_side_effects=True, vmem_limit_bytes=48 * 2**20
@@ -453,19 +470,13 @@
     requests = lax.dynamic_slice_in_dim(request_rows[0], core * share, share, 1)
     fetched = fetch_rows(source, requests[:, None, :]).reshape(2 * tiles * quarter, LANES)
 
-    slots = lax.dynamic_slice_in_dim(cell_slots[0], core * cells_half, cells_half, 1)
     counts = lax.dynamic_slice_in_dim(cell_counts[0], core * cells_half, cells_half, 1)
-    owner, place = slots // slots_each, slots % slots_each
-    served, inside = place // share, place % share
-    part = tiles * quarter
-    table_rows = (inside // quarter) * (2 * part) + served * part + owner * quarter + inside % quarter
-    def arrange(weights):
-        return jnp.transpose(weights, (0, 1, 3, 2)).reshape(9, weights.shape[3], weights.shape[2])
-
-    bias_rows = jnp.broadcast_to(bias_first[None], (8, bias_first.shape[0]))
+    def taps(weights):
+        return weights.reshape(9, weights.shape[2], weights.shape[3])
+
     return conv_block(
-        table_rows.T.reshape(-1), counts.astype(F32).T, fetched, seam,
-        arrange(conv_first), bias_rows, arrange(conv_second), bias_second[None],
+        slots_each, cell_slots[0], counts.astype(F32).T, fetched, seam,
+        taps(conv_first), bias_first[None], taps(conv_second), bias_second[None],
     )[None]
 
 

time: 84.4 us -> 82.7 us (0.980)
  local copies, waits for them, and re-layouts: 6.51 us -> 2.73 us
  Pallas kernels: 76.5 us -> 79.6 us
  other arithmetic: 1.02 us -> 0.07 us
    pallas_call x1, Pallas kernels: 34 us -> 37.1 us  [conv_block(): pl.pallas_call(kernel, out_shape=jax.ShapeDtypeStruct((chans // 2, 2 * ce...]
    transpose x3 -> x0, local copies, waits for them, and re-layouts: 2.54 us -> none  [the longest x2 2.18 us: arrange(): jnp.transpose(weights, (0, 1, 3, 2))]
    transpose x1 -> x0, other arithmetic: 0.95 us -> none  [shards(): table_rows.T.reshape(-1)]
    unnamed x9 -> x17, local copies, waits for them, and re-layouts: 1.88 us -> 1.94 us
where the time goes in v5:
time: 82.7 us; the launch traced here: 82.5 us
  Pallas kernels  79.6 us (96%)
  local copies, waits for them, and re-layouts  2.73 us (3%)
    pallas_call x1, Pallas kernels, fetch_rows(): pl.pallas_call(fetch_kernel, out_shape=jax.ShapeDtypeStruct((2, tiles, qu...  42.5 us
    pallas_call x1, Pallas kernels, conv_block(): pl.pallas_call(kernel, out_shape=jax.ShapeDtypeStruct((chans // 2, 2 * ce...  37.1 us
    unnamed x17, local copies, waits for them, and re-layouts  1.94 us

profile of v5, /device:TPU:0, one launch (start us, length us, event | category | flops | bytes accessed | tf_op | source)
XLA Modules:
  0.0 82.5 jit_solution(4614240354226144322)
XLA Ops:
  0.0 0.0 copy-start
  0.0 0.0 copy-start.1
  0.0 0.8 copy.11.refs_3_
  0.8 0.0 copy-done
  0.9 0.8 constant_dynamic-slice_fusion.1
  1.6 0.4 copy.12
  2.0 0.0 copy-start.2
  2.0 0.0 copy-start.3
  2.0 0.0 copy-start.4
  2.0 0.0 copy-start.5
  2.1 0.0 copy-start.6
  2.1 0.1 convert_bitcast_fusion.refs_1_
  2.1 0.0 copy-done.1
  2.2 42.5 %fetch_rows.1 = bf16[2,8,512,128]{3,2,1,0:T(8,128)(2,1)S(1)} custom-call(bf16[32,8192]{1,0:T(8,128)(2,1)S(1)} %copy-done.1, s32[8,1,1024]{2,1,0:T(1,128)S(1)} %broadcast_in_dim.12.wanted_ref), custom_call_target="tpu_custom_call" | custom-call | tf_op jit(solution)/shard_map/fetch_rows/pallas_call | solution.py:165
  44.6 0.0 copy-done.2
  44.6 0.0 copy-done.3
  44.6 0.0 copy-done.4
  44.7 0.0 copy-done.5
  44.7 0.0 copy-done.6
  44.7 37.1 %conv_block.1 = bf16[32,4096]{1,0:T(8,128)(2,1)S(1)} custom-call(s32[4,4096]{1,0:T(4,128)S(1)} %bitcast.15, f32[2048,4]{1,0:T(8,128)S(1)} %convert_bitcast_fusion.refs_1_, bf16[8192,128]{1,0:T(8,128)(2,1)S(1)} %bitcast.11, s32[8,4]{1,0:T(8,128)S(1)} %copy.11.refs_3_, bf16[9,64,64]{2,1,0:T(8,128)(2,1)S(1)} %bitcast.13, f32[1,64]{1,0:T(1,128)S(1)} %bitcast.16, ...), custom_call_target="tpu_custom_call" | custom-call | tf_op jit(solution)/shard_map/conv_block/pallas_call | solution.py:434
  81.8 0.7 copy.14
  (2 shorter events, 0.0 us)
Async XLA Ops:
  0.0 0.8 %copy-start = (s32[1,8,2048]{2,1,0:T(8,128)S(1)}, s32[1,8,2048]{2,1,0:T(8,128)}, u32[]{:S(2)}) copy-start(s32[1,8,2048]{2,1,0:T(8,128)} %param.10) | copy-start | bytes 196612
  0.0 2.1 %copy-start.1 = (bf16[32,8192]{1,0:T(8,128)(2,1)S(1)}, bf16[32,8192]{1,0:T(8,128)(2,1)}, u32[]{:S(2)}) copy-start(bf16[32,8192]{1,0:T(8,128)(2,1)} %source_ref.1) | copy-start | bytes 1572868
  2.0 42.6 %copy-start.2 = (bf16[3,3,64,64]{3,2,1,0:T(8,128)(2,1)S(1)}, bf16[3,3,64,64]{3,2,1,0:T(8,128)(2,1)}, u32[]{:S(2)}) copy-start(bf16[3,3,64,64]{3,2,1,0:T(8,128)(2,1)} %param.14) | copy-start | bytes 221188
  2.0 42.6 %copy-start.3 = (bf16[3,3,64,128]{3,2,1,0:T(8,128)(2,1)S(1)}, bf16[3,3,64,128]{3,2,1,0:T(8,128)(2,1)}, u32[]{:S(2)}) copy-start(bf16[3,3,64,128]{3,2,1,0:T(8,128)(2,1)} %param.16) | copy-start | bytes 442372
  2.0 42.6 %copy-start.4 = (s32[1,4,4096]{2,1,0:T(4,128)S(1)}, s32[1,4,4096]{2,1,0:T(4,128)}, u32[]{:S(2)}) copy-start(s32[1,4,4096]{2,1,0:T(4,128)} %param.11) | copy-start | bytes 196612
  2.0 42.6 %copy-start.5 = (f32[64]{0:T(128)S(1)}, f32[64]{0:T(128)}, u32[]{:S(2)}) copy-start(f32[64]{0:T(128)} %param.15) | copy-start | bytes 772
  2.1 42.6 %copy-start.6 = (f32[64]{0:T(128)S(1)}, f32[64]{0:T(128)}, u32[]{:S(2)}) copy-start(f32[64]{0:T(128)} %param.17) | copy-start | bytes 772

commit v6 on v5

--- a/solution.py
+++ b/solution.py
@@ -204,7 +204,7 @@
             first = base + g * 8
             for u in range(8):
                 for k in range(entries):
-                    rows_ref[k, pl.ds(g * 8 + u, 1), :] = table_ref[pl.ds(slots_here[k, 0, first + u], 1), :]
+                    rows_ref[k, pl.ds(g * 8 + u, 1), :] = table_ref[pl.ds(slots_here[first + (k * cells + u)], 1), :]
             return inner
 
         lax.fori_loop(0, chunk // 8, group, 0)
@@ -267,7 +267,7 @@
     group, inside = inside // (cap // 4), inside % (cap // 4)
     at_row = group * part + served * (part // 2) + owner * (cap // 4) + inside
     for k in range(slots_ref.shape[0]):
-        slots_moved[k] = at_row[k : k + 1]
+        slots_moved[k * cells : (k + 1) * cells] = at_row[k]
     slots_copy = pltpu.make_async_copy(slots_moved, slots_here, side_sems.at[6])
     slots_copy.start()
     for other in targets:
@@ -438,8 +438,8 @@
         out_specs=VMEM,
         scratch_shapes=[
             shape((2 * fetched.shape[0], LANES), F32), shape((entries, 128, LANES), F32),
-            shape((4 * SIDE, pack), BF), shape((entries, 1, cells), jnp.int32),
-            pltpu.SMEM((entries, 1, cells), jnp.int32), shape((9, hid, chans), BF),
+            shape((4 * SIDE, pack), BF), shape((entries * cells,), jnp.int32),
+            pltpu.SMEM((entries * cells,), jnp.int32), shape((9, hid, chans), BF),
             shape((rows + 16, chans), F32), shape((rows + 16, hid), F32),
             shape((SIDE + 16, hid), F32), shape((SIDE + 16, hid), F32),
             shape((rows, chans), F32), shape((rows, hid), F32),

time: 82.7 us -> 79.3 us (0.959)
  Pallas kernels: 79.6 us -> 76.2 us
    pallas_call x1, Pallas kernels: 37.1 us -> 33.7 us  [conv_block(): pl.pallas_call(kernel, out_shape=jax.ShapeDtypeStruct((chans // 2, 2 * ce...]
where the time goes in v6:
time: 79.3 us; the launch traced here: 79.1 us
  Pallas kernels  76.2 us (96%)
  local copies, waits for them, and re-layouts  2.73 us (3%)
    pallas_call x1, Pallas kernels, fetch_rows(): pl.pallas_call(fetch_kernel, out_shape=jax.ShapeDtypeStruct((2, tiles, qu...  42.5 us
    pallas_call x1, Pallas kernels, conv_block(): pl.pallas_call(kernel, out_shape=jax.ShapeDtypeStruct((chans // 2, 2 * ce...  33.7 us
    unnamed x17, local copies, waits for them, and re-layouts  1.94 us

profile of v6, /device:TPU:0, one launch (start us, length us, event | category | flops | bytes accessed | tf_op | source)
XLA Modules:
  0.0 79.1 jit_solution(16531951490264262074)
XLA Ops:
  0.0 0.0 copy-start
  0.0 0.0 copy-start.1
  0.0 0.8 %copy.11.refs_3_ = s32[8,4]{1,0:T(8,128)S(1)} copy(s32[8,4]{0,1:T(4,128)} %param.13) | data formatting | bytes 256 | tf_op args[4]
  0.8 0.0 copy-done
  0.9 0.8 constant_dynamic-slice_fusion.1
  1.6 0.4 copy.12
  2.0 0.0 copy-start.2
  2.0 0.0 copy-start.3
  2.0 0.0 copy-start.4
  2.0 0.0 copy-start.5
  2.1 0.0 copy-start.6
  2.1 0.1 convert_bitcast_fusion.refs_1_
  2.1 0.0 copy-done.1
  2.2 42.5 %fetch_rows.1 = bf16[2,8,512,128]{3,2,1,0:T(8,128)(2,1)S(1)} custom-call(bf16[32,8192]{1,0:T(8,128)(2,1)S(1)} %copy-done.1, s32[8,1,1024]{2,1,0:T(1,128)S(1)} %broadcast_in_dim.12.wanted_ref), custom_call_target="tpu_custom_call" | custom-call | tf_op jit(solution)/shard_map/fetch_rows/pallas_call | solution.py:165
  44.6 0.0 copy-done.2
  44.6 0.0 copy-done.3
  44.6 0.0 copy-done.4
  44.7 0.0 copy-done.5
  44.7 0.0 copy-done.6
  44.7 33.7 %conv_block.1 = bf16[32,4096]{1,0:T(8,128)(2,1)S(1)} custom-call(s32[4,4096]{1,0:T(4,128)S(1)} %bitcast.15, f32[2048,4]{1,0:T(8,128)S(1)} %convert_bitcast_fusion.refs_1_, bf16[8192,128]{1,0:T(8,128)(2,1)S(1)} %bitcast.11, s32[8,4]{1,0:T(8,128)S(1)} %copy.11.refs_3_, bf16[9,64,64]{2,1,0:T(8,128)(2,1)S(1)} %bitcast.13, f32[1,64]{1,0:T(1,128)S(1)} %bitcast.16, ...), custom_call_target="tpu_custom_call" | custom-call | tf_op jit(solution)/shard_map/conv_block/pallas_call | solution.py:434
  78.4 0.7 copy.14
  (2 shorter events, 0.0 us)
Async XLA Ops:
  0.0 0.8 %copy-start = (s32[1,8,2048]{2,1,0:T(8,128)S(1)}, s32[1,8,2048]{2,1,0:T(8,128)}, u32[]{:S(2)}) copy-start(s32[1,8,2048]{2,1,0:T(8,128)} %param.10) | copy-start | bytes 196612
  0.0 2.1 %copy-start.1 = (bf16[32,8192]{1,0:T(8,128)(2,1)S(1)}, bf16[32,8192]{1,0:T(8,128)(2,1)}, u32[]{:S(2)}) copy-start(bf16[32,8192]{1,0:T(8,128)(2,1)} %source_ref.1) | copy-start | bytes 1572868
  2.0 42.6 %copy-start.2 = (bf16[3,3,64,64]{3,2,1,0:T(8,128)(2,1)S(1)}, bf16[3,3,64,64]{3,2,1,0:T(8,128)(2,1)}, u32[]{:S(2)}) copy-start(bf16[3,3,64,64]{3,2,1,0:T(8,128)(2,1)} %param.14) | copy-start | bytes 221188
  2.0 42.6 %copy-start.3 = (bf16[3,3,64,128]{3,2,1,0:T(8,128)(2,1)S(1)}, bf16[3,3,64,128]{3,2,1,0:T(8,128)(2,1)}, u32[]{:S(2)}) copy-start(bf16[3,3,64,128]{3,2,1,0:T(8,128)(2,1)} %param.16) | copy-start | bytes 442372
  2.0 42.6 %copy-start.4 = (s32[1,4,4096]{2,1,0:T(4,128)S(1)}, s32[1,4,4096]{2,1,0:T(4,128)}, u32[]{:S(2)}) copy-start(s32[1,4,4096]{2,1,0:T(4,128)} %param.11) | copy-start | bytes 196612
  2.0 42.6 %copy-start.5 = (f32[64]{0:T(128)S(1)}, f32[64]{0:T(128)}, u32[]{:S(2)}) copy-start(f32[64]{0:T(128)} %param.15) | copy-start | bytes 772
  2.1 42.6 %copy-start.6 = (f32[64]{0:T(128)S(1)}, f32[64]{0:T(128)}, u32[]{:S(2)}) copy-start(f32[64]{0:T(128)} %param.17) | copy-start | bytes 772
